TPU v7x, 32 devices: a whole 2x2x4 slice. The times are simulated.
32 devices in a mesh: shard: 4 (over x, core), ctx: 2 (over y), tp: 4 (over z).
Axes of the slice: x: 2, y: 2, z: 4, core: 2. Of those that a mesh axis runs over, the one named last changes fastest.
Arguments:
- tokens: bfloat16 [4096, 960], P(('shard', 'ctx', 'tp')), may hold values from -6 to 6
- positions: int32 [4096], P('shard'), may hold values from 0 to 1023, as said below
- norm1_gain: bfloat16 [960], P('shard'), may hold values from 0.25 to 1.75
- w_query: bfloat16 [960, 960], P('shard'), may hold values from -0.1875 to 0.1875
- w_key: bfloat16 [960, 320], P('shard'), may hold values from -0.1875 to 0.1875
- w_value: bfloat16 [960, 320], P('shard'), may hold values from -0.1875 to 0.1875
- w_out: bfloat16 [960, 960], P('shard'), may hold values from -6 to 6
- norm2_gain: bfloat16 [960], P('shard'), may hold values from 0.25 to 1.75
- w_gate: bfloat16 [960, 2560], P('shard', 'tp'), may hold values from -0.1875 to 0.1875
- w_up: bfloat16 [960, 2560], P('shard', 'tp'), may hold values from -0.1875 to 0.1875
- w_down: bfloat16 [2560, 960], P('tp', 'shard'), may hold values from -0.125 to 0.125
- out_grad: bfloat16 [4096, 960], P(('shard', 'ctx', 'tp')), may hold values from -6 to 6
Outputs:
- result: bfloat16 [4096, 960], P(('shard', 'ctx', 'tp'))
- tokens_grad: bfloat16 [4096, 960], P(('shard', 'ctx', 'tp'))
- norm1_gain_grad: float32 [960], P('shard')
- w_query_grad: float32 [960, 960], P('shard')
- w_key_grad: float32 [960, 320], P('shard')
- w_value_grad: float32 [960, 320], P('shard')
- w_out_grad: float32 [960, 960], P('shard')
- norm2_gain_grad: float32 [960], P('shard')
- w_gate_grad: float32 [960, 2560], P('shard', 'tp')
- w_up_grad: float32 [960, 2560], P('shard', 'tp')
- w_down_grad: float32 [2560, 960], P('tp', 'shard')
Inputs may be any that keep to these rules, and one draw needn't show every extreme that they name: `positions`: in each sequence every place 0 to 1023 appears once. The sequence consists of 4 blocks of 256 places; its rows run over the ctx ranks, within a rank over the tp ranks, then over two halves of 64 rows each. Rank c holds in its first half block b_c and in its second half block 3 - b_c, where b is a permutation of 0 to 1 drawn for each sequence; tp rank t holds places t * 64 to t * 64 + 63 of each of these blocks, in order.
All inputs are finite; a program needn't handle non-finite values.
Results may differ from a plain program's by a relative error of at most 0.025.
Values may be sent and summed in bfloat16 or wider, within the bound.
A program may use at most 128 MiB of HBM per device.

v0:
```python
import math

import jax
import jax.numpy as jnp
from jax import lax
from jax.sharding import PartitionSpec as P

QUERY_HEADS = 15
KEY_VALUE_HEADS = 5
HEAD_SIZE = 64


norm_eps = 1e-05
rope_base = 100000.0
negative_large = -1e30


def rope_tables(block_places, head_width):
    half_width = head_width // 2
    frequency = rope_base ** (-(jnp.arange(half_width, dtype=jnp.float32) * 2.0 / head_width))
    angles = block_places.astype(jnp.float32)[:, None] * frequency[None, :]
    return (jnp.cos(angles), jnp.sin(angles))


def apply_rotary(heads, cosine_table, sine_table):
    half_width = heads.shape[-1] // 2
    first = heads[..., :half_width]
    second = heads[..., half_width:]
    cosine_rows = cosine_table[:, None, :]
    sine_rows = sine_table[:, None, :]
    return jnp.concatenate(
        [first * cosine_rows - second * sine_rows, second * cosine_rows + first * sine_rows],
        axis=-1,
    )


def norm_rows(rows):
    inverse = lax.rsqrt(jnp.mean(rows * rows, axis=-1, keepdims=True) + norm_eps)
    return (rows * inverse, inverse)


def norm_back(grad_normed, normed, inverse, gain):
    scaled = grad_normed * gain
    grad_rows = inverse * (scaled - normed * jnp.mean(scaled * normed, axis=-1, keepdims=True))
    return (grad_rows, jnp.sum(grad_normed * normed, axis=0))


def per_device(
    tokens,
    positions,
    norm1_gain,
    w_query,
    w_key,
    w_value,
    w_out,
    norm2_gain,
    w_gate,
    w_up,
    w_down,
    out_grad,
):
    gain_one, query_w, key_w, value_weight, out_w, gain_two, gate_w, up_w, down_w = (
        lax.all_gather(norm1_gain, "shard", axis=0, tiled=True),
        lax.all_gather(w_query, "shard", axis=0, tiled=True),
        lax.all_gather(w_key, "shard", axis=0, tiled=True),
        lax.all_gather(w_value, "shard", axis=0, tiled=True),
        lax.all_gather(w_out, "shard", axis=0, tiled=True),
        lax.all_gather(norm2_gain, "shard", axis=0, tiled=True),
        lax.all_gather(w_gate, "shard", axis=0, tiled=True),
        lax.all_gather(w_up, "shard", axis=0, tiled=True),
        lax.all_gather(w_down, "shard", axis=1, tiled=True),
    )
    shard_rows = tokens.shape[0]
    width = tokens.shape[1]
    seq_len = positions.shape[0]
    query_groups = QUERY_HEADS // KEY_VALUE_HEADS
    key_value_width = KEY_VALUE_HEADS * HEAD_SIZE
    head_scale = 1.0 / math.sqrt(HEAD_SIZE)
    gain_one = gain_one.astype(jnp.float32)
    gain_two = gain_two.astype(jnp.float32)
    group_rank = lax.axis_index("ctx") * lax.axis_size("tp") + lax.axis_index("tp")
    own_place = lax.dynamic_slice_in_dim(positions, group_rank * shard_rows, shard_rows)
    residual = tokens.astype(jnp.float32)
    normed_one, inverse_one = norm_rows(residual)
    first_hidden = (normed_one * gain_one).astype(jnp.bfloat16)
    unrotated_query = jnp.dot(first_hidden, query_w, preferred_element_type=jnp.float32)
    unrotated_key = jnp.dot(first_hidden, key_w, preferred_element_type=jnp.float32)
    value_rows = jnp.dot(first_hidden, value_weight, preferred_element_type=jnp.float32).astype(
        jnp.bfloat16
    )
    cosine_table, sine_table = rope_tables(own_place, HEAD_SIZE)
    query_tensor = apply_rotary(
        unrotated_query.reshape(shard_rows, QUERY_HEADS, HEAD_SIZE), cosine_table, sine_table
    ).astype(jnp.bfloat16)
    query_tensor = query_tensor.reshape(shard_rows, KEY_VALUE_HEADS, query_groups, HEAD_SIZE)
    key_row_list = apply_rotary(
        unrotated_key.reshape(shard_rows, KEY_VALUE_HEADS, HEAD_SIZE), cosine_table, sine_table
    ).astype(jnp.bfloat16)
    key_row_list = key_row_list.reshape(shard_rows, key_value_width)
    gathered_keys, gathered_values = (
        lax.all_gather(key_row_list, ("ctx", "tp"), axis=0, tiled=True),
        lax.all_gather(value_rows, ("ctx", "tp"), axis=0, tiled=True),
    )
    block_size = 512
    pair_count = seq_len // block_size
    blocked_keys = gathered_keys.reshape(pair_count, block_size, KEY_VALUE_HEADS, HEAD_SIZE)
    blocked_values = gathered_values.reshape(pair_count, block_size, KEY_VALUE_HEADS, HEAD_SIZE)
    place_blocks = positions.reshape(pair_count, block_size)

    def forward_block(carry, items):
        run_max, run_total, run_acc = carry
        key_block, value_block, key_place = items
        allowed = key_place[None, :] <= own_place[:, None]
        scores = (
            jnp.einsum(
                "qhgd,khd->hgqk", query_tensor, key_block, preferred_element_type=jnp.float32
            )
            * head_scale
        )
        scores = jnp.where(allowed, scores, negative_large)
        new_max = jnp.maximum(run_max, jnp.max(scores, axis=-1))
        weights = jnp.where(allowed, jnp.exp(scores - new_max[..., None]), 0.0)
        factor = jnp.exp(run_max - new_max)
        run_total = run_total * factor + jnp.sum(weights, axis=-1)
        run_acc = run_acc * factor[..., None] + jnp.einsum(
            "hgqk,khd->hgqd",
            weights.astype(jnp.bfloat16),
            value_block,
            preferred_element_type=jnp.float32,
        )
        return ((new_max, run_total, run_acc), None)

    start_carry = (
        jnp.full((KEY_VALUE_HEADS, query_groups, shard_rows), negative_large, jnp.float32),
        jnp.zeros((KEY_VALUE_HEADS, query_groups, shard_rows), jnp.float32),
        jnp.zeros((KEY_VALUE_HEADS, query_groups, shard_rows, HEAD_SIZE), jnp.float32),
    )
    (run_max, run_total, run_acc), _ = lax.scan(
        forward_block, start_carry, (blocked_keys, blocked_values, place_blocks)
    )
    log_total = run_max + jnp.log(run_total)
    attention_output = jnp.transpose(run_acc / run_total[..., None], (2, 0, 1, 3))
    attention_low = attention_output.reshape(shard_rows, width).astype(jnp.bfloat16)
    middle = residual + jnp.dot(attention_low, out_w, preferred_element_type=jnp.float32)
    normed_two, inverse_two = norm_rows(middle)
    hidden_two = (normed_two * gain_two).astype(jnp.bfloat16)
    mlp_input = lax.all_gather(hidden_two, "tp", axis=0, tiled=True)
    gate = jnp.dot(mlp_input, gate_w, preferred_element_type=jnp.float32)
    upper = jnp.dot(mlp_input, up_w, preferred_element_type=jnp.float32)
    sigma = jax.nn.sigmoid(gate)
    active = gate * sigma
    inner = (active * upper).astype(jnp.bfloat16)
    mlp_output = lax.psum_scatter(
        jnp.dot(inner, down_w, preferred_element_type=jnp.float32).astype(jnp.bfloat16),
        "tp",
        scatter_dimension=0,
        tiled=True,
    ).astype(jnp.float32)
    result = (middle + mlp_output).astype(jnp.bfloat16)
    grad_all = lax.all_gather(out_grad, "tp", axis=0, tiled=True)
    grad_inner = jnp.einsum("rd,fd->rf", grad_all, down_w, preferred_element_type=jnp.float32)
    grad_down_w = jnp.einsum("rf,rd->fd", inner, grad_all, preferred_element_type=jnp.float32)
    grad_gate = (grad_inner * upper * sigma * (1.0 + gate * (1.0 - sigma))).astype(jnp.bfloat16)
    grad_upper = (grad_inner * active).astype(jnp.bfloat16)
    grad_gate_w = jnp.einsum("rd,rf->df", mlp_input, grad_gate, preferred_element_type=jnp.float32)
    grad_up_w = jnp.einsum("rd,rf->df", mlp_input, grad_upper, preferred_element_type=jnp.float32)
    grad_hidden_two = lax.psum_scatter(
        (
            jnp.einsum("rf,df->rd", grad_gate, gate_w, preferred_element_type=jnp.float32)
            + jnp.einsum("rf,df->rd", grad_upper, up_w, preferred_element_type=jnp.float32)
        ).astype(jnp.bfloat16),
        "tp",
        scatter_dimension=0,
        tiled=True,
    ).astype(jnp.float32)
    shard_gate, shard_up, shard_down = (
        lax.psum_scatter(
            grad_gate_w.astype(jnp.bfloat16), "shard", scatter_dimension=0, tiled=True
        ).astype(jnp.float32),
        lax.psum_scatter(
            grad_up_w.astype(jnp.bfloat16), "shard", scatter_dimension=0, tiled=True
        ).astype(jnp.float32),
        lax.psum_scatter(
            grad_down_w.astype(jnp.bfloat16), "shard", scatter_dimension=1, tiled=True
        ).astype(jnp.float32),
    )
    out_gate, out_up, out_down = (
        lax.psum(shard_gate.astype(jnp.bfloat16), "ctx").astype(jnp.float32),
        lax.psum(shard_up.astype(jnp.bfloat16), "ctx").astype(jnp.float32),
        lax.psum(shard_down.astype(jnp.bfloat16), "ctx").astype(jnp.float32),
    )
    grad_middle_norm, grad_gain_two = norm_back(grad_hidden_two, normed_two, inverse_two, gain_two)
    grad_middle = out_grad.astype(jnp.float32) + grad_middle_norm
    grad_middle_low = grad_middle.astype(jnp.bfloat16)
    grad_out_w = jnp.einsum(
        "rc,rd->cd", attention_low, grad_middle_low, preferred_element_type=jnp.float32
    )
    attention_gradient = jnp.einsum(
        "rd,cd->rc", grad_middle_low, out_w, preferred_element_type=jnp.float32
    )
    attention_gradient = attention_gradient.astype(jnp.bfloat16).reshape(
        shard_rows, KEY_VALUE_HEADS, query_groups, HEAD_SIZE
    )
    delta = jnp.einsum("qhgd,qhgd->hgq", attention_gradient.astype(jnp.float32), attention_output)

    def score_grads(key_block, value_block, key_place):
        allowed = key_place[None, :] <= own_place[:, None]
        scores = (
            jnp.einsum(
                "qhgd,khd->hgqk", query_tensor, key_block, preferred_element_type=jnp.float32
            )
            * head_scale
        )
        scores = jnp.where(allowed, scores, negative_large)
        weights = jnp.where(allowed, jnp.exp(scores - log_total[..., None]), 0.0)
        grad_weights = jnp.einsum(
            "qhgd,khd->hgqk", attention_gradient, value_block, preferred_element_type=jnp.float32
        )
        grad_scores = (weights * (grad_weights - delta[..., None])).astype(jnp.bfloat16)
        return (weights.astype(jnp.bfloat16), grad_scores)

    def key_value_terms(weights_low, grad_scores):
        grad_key = (
            jnp.einsum(
                "hgqk,qhgd->khd", grad_scores, query_tensor, preferred_element_type=jnp.float32
            )
            * head_scale
        )
        grad_value = jnp.einsum(
            "hgqk,qhgd->khd", weights_low, attention_gradient, preferred_element_type=jnp.float32
        )
        return (grad_key, grad_value)

    def query_term(grad_scores, key_block):
        return (
            jnp.einsum("hgqk,khd->qhgd", grad_scores, key_block, preferred_element_type=jnp.float32)
            * head_scale
        )

    query_offset = jnp.zeros((shard_rows, KEY_VALUE_HEADS, query_groups, HEAD_SIZE), jnp.float32)

    def backward_block(grad_query, items):
        key_block, value_block, key_place = items
        weights_low, grad_scores = score_grads(key_block, value_block, key_place)
        grad_key, grad_value = key_value_terms(weights_low, grad_scores)
        return (grad_query + query_term(grad_scores, key_block), (grad_key, grad_value))

    grad_query, (key_terms, value_terms) = lax.scan(
        backward_block, query_offset, (blocked_keys, blocked_values, place_blocks)
    )
    local_key_gradient, grad_value_own = (
        lax.psum_scatter(
            key_terms.reshape(seq_len, key_value_width).astype(jnp.bfloat16),
            ("ctx", "tp"),
            scatter_dimension=0,
            tiled=True,
        ).astype(jnp.float32),
        lax.psum_scatter(
            value_terms.reshape(seq_len, key_value_width).astype(jnp.bfloat16),
            ("ctx", "tp"),
            scatter_dimension=0,
            tiled=True,
        ).astype(jnp.float32),
    )
    grad_query_raw = (
        apply_rotary(
            grad_query.reshape(shard_rows, QUERY_HEADS, HEAD_SIZE), cosine_table, -sine_table
        )
        .astype(jnp.bfloat16)
        .reshape(shard_rows, width)
    )
    grad_key_raw = (
        apply_rotary(
            local_key_gradient.reshape(shard_rows, KEY_VALUE_HEADS, HEAD_SIZE),
            cosine_table,
            -sine_table,
        )
        .astype(jnp.bfloat16)
        .reshape(shard_rows, key_value_width)
    )
    grad_value_low = grad_value_own.astype(jnp.bfloat16)
    grad_query_w = jnp.einsum(
        "rd,rc->dc", first_hidden, grad_query_raw, preferred_element_type=jnp.float32
    )
    grad_key_w = jnp.einsum(
        "rd,rc->dc", first_hidden, grad_key_raw, preferred_element_type=jnp.float32
    )
    grad_value_w = jnp.einsum(
        "rd,rc->dc", first_hidden, grad_value_low, preferred_element_type=jnp.float32
    )
    grad_hidden_one = (
        jnp.einsum("rc,dc->rd", grad_query_raw, query_w, preferred_element_type=jnp.float32)
        + jnp.einsum("rc,dc->rd", grad_key_raw, key_w, preferred_element_type=jnp.float32)
        + jnp.einsum("rc,dc->rd", grad_value_low, value_weight, preferred_element_type=jnp.float32)
    )
    grad_residual_norm, grad_gain_one = norm_back(
        grad_hidden_one, normed_one, inverse_one, gain_one
    )
    tokens_grad = (grad_middle + grad_residual_norm).astype(jnp.bfloat16)
    shard_gain_one, shard_query, shard_key, shard_value, shard_out, shard_gain_two = (
        lax.psum_scatter(
            grad_gain_one.astype(jnp.bfloat16), "shard", scatter_dimension=0, tiled=True
        ).astype(jnp.float32),
        lax.psum_scatter(
            grad_query_w.astype(jnp.bfloat16), "shard", scatter_dimension=0, tiled=True
        ).astype(jnp.float32),
        lax.psum_scatter(
            grad_key_w.astype(jnp.bfloat16), "shard", scatter_dimension=0, tiled=True
        ).astype(jnp.float32),
        lax.psum_scatter(
            grad_value_w.astype(jnp.bfloat16), "shard", scatter_dimension=0, tiled=True
        ).astype(jnp.float32),
        lax.psum_scatter(
            grad_out_w.astype(jnp.bfloat16), "shard", scatter_dimension=0, tiled=True
        ).astype(jnp.float32),
        lax.psum_scatter(
            grad_gain_two.astype(jnp.bfloat16), "shard", scatter_dimension=0, tiled=True
        ).astype(jnp.float32),
    )
    out_gain_one, out_query, out_key, out_value, out_proj, out_gain_two = (
        lax.psum(shard_gain_one.astype(jnp.bfloat16), ("ctx", "tp")).astype(jnp.float32),
        lax.psum(shard_query.astype(jnp.bfloat16), ("ctx", "tp")).astype(jnp.float32),
        lax.psum(shard_key.astype(jnp.bfloat16), ("ctx", "tp")).astype(jnp.float32),
        lax.psum(shard_value.astype(jnp.bfloat16), ("ctx", "tp")).astype(jnp.float32),
        lax.psum(shard_out.astype(jnp.bfloat16), ("ctx", "tp")).astype(jnp.float32),
        lax.psum(shard_gain_two.astype(jnp.bfloat16), ("ctx", "tp")).astype(jnp.float32),
    )
    return (
        result,
        tokens_grad,
        out_gain_one,
        out_query,
        out_key,
        out_value,
        out_proj,
        out_gain_two,
        out_gate,
        out_up,
        out_down,
    )


def solution(mesh):
    in_specs = (
        P(("shard", "ctx", "tp"), None),
        P("shard"),
        P("shard"),
        P("shard", None),
        P("shard", None),
        P("shard", None),
        P("shard", None),
        P("shard"),
        P("shard", "tp"),
        P("shard", "tp"),
        P("tp", "shard"),
        P(("shard", "ctx", "tp"), None),
    )
    out_specs = (
        P(("shard", "ctx", "tp"), None),
        P(("shard", "ctx", "tp"), None),
        P("shard"),
        P("shard", None),
        P("shard", None),
        P("shard", None),
        P("shard", None),
        P("shard"),
        P("shard", "tp"),
        P("shard", "tp"),
        P("tp", "shard"),
    )
    return jax.shard_map(
        per_device, mesh=mesh, in_specs=in_specs, out_specs=out_specs, check_vma=False
    )
```

profile of v0, /device:TPU:20, one launch (start us, length us, event | category | flops | bytes accessed | tf_op | source)
XLA Modules:
  0.0 732.8 jit_solution(1210442091201877924)
XLA Ops:
  13.7 6.9 all-reduce.7
  20.7 11.5 %all-gather = bf16[4,240,320]{1,2,0:T(8,128)(2,1)S(1)} all-gather(bf16[1,240,320]{1,2,0:T(8,128)(2,1)S(1)} %bitcast.250), channel_id=1, replica_groups=mesh['shard'=4,'ctx'=2,'tp'=4] {'shard'}, dimensions={0}, use_global_device_ids=true | all-gather | bytes 768000 | tf_op jit(solution)/shard_map/all_gather | solution.py:65
  34.1 27.4 %all_gather.41 = bf16[1024,320]{0,1:T(8,128)(2,1)S(1)} all-gather(bf16[128,320]{0,1:T(8,128)(2,1)S(1)} %bitcast.246), channel_id=1, replica_groups=mesh['shard'=4,'ctx'=2,'tp'=4] {'ctx','tp'}, dimensions={0}, use_global_device_ids=true | all-gather | bytes 737280 | tf_op jit(solution)/shard_map/all_gather | solution.py:101
  62.1 7.2 all-gather.1
  70.9 29.9 %all_gather.44 = bf16[1024,320]{0,1:T(8,128)(2,1)S(1)} all-gather(bf16[128,320]{0,1:T(8,128)(2,1)S(1)} %convolution_convert_fusion.9), channel_id=1, replica_groups=mesh['shard'=4,'ctx'=2,'tp'=4] {'ctx','tp'}, dimensions={0}, use_global_device_ids=true | all-gather | bytes 737280 | tf_op jit(solution)/shard_map/all_gather | solution.py:102
  102.1 19.2 %all_gather.51 = bf16[512,960]{0,1:T(8,128)(2,1)} all-gather(bf16[128,960]{0,1:T(8,128)(2,1)S(1)} %copy-done.13), channel_id=1, replica_groups=mesh['shard'=4,'ctx'=2,'tp'=4] {'tp'}, dimensions={0}, use_global_device_ids=true | all-gather | bytes 1228800 | tf_op jit(solution)/shard_map/all_gather | solution.py:160
  124.1 14.6 %while.30 = (s32[]{:T(128)}, f32[5,3,128]{2,1,0:T(4,128)S(1)}, f32[5,3,128]{2,1,0:T(4,128)S(1)}, f32[5,3,128,64]{2,3,1,0:T(8,128)S(1)}, s32[2,512]{1,0:T(2,128)S...) while((s32[]{:T(128)}, f32[5,3,128]{2,1,0:T(4,128)S(1)}, ...), condition=%wide.region_4.5_spmd.clone, body=%wide.region_1.4_spmd.clone.sunk | while | flops 264881536 | bytes 32427708 | solution.py:138
  141.5 18.7 %all_gather.47 = bf16[512,960]{0,1:T(8,128)(2,1)} all-gather(bf16[128,960]{0,1:T(8,128)(2,1)S(1)} %multiply_convert_fusion.3), channel_id=1, replica_groups=mesh['shard'=4,'ctx'=2,'tp'=4] {'tp'}, dimensions={0}, use_global_device_ids=true | all-gather | bytes 1228800 | tf_op jit(solution)/shard_map/all_gather | solution.py:147
  184.2 21.0 %reduce-scatter.36.cloned.1.call-done = bf16[128,960]{1,0:T(8,128)(2,1)} async-done(((bf16[512,960]{1,0:T(8,128)(2,1)}), bf16[128,960]{1,0:T(8,128)(2,1)}) %reduce-scatter.36.cloned.1.call-update) | async-done | bytes 245776
  206.7 26.7 %reduce-scatter.34.cloned.1.call-done = bf16[128,960]{1,0:T(8,128)(2,1)} async-done(((bf16[512,960]{1,0:T(8,128)(2,1)}), bf16[128,960]{1,0:T(8,128)(2,1)}) %reduce-scatter.34.cloned.1.call-update) | async-done | bytes 245776
  237.0 19.9 %while.31 = (s32[]{:T(128)}, f32[128,5,3,64]{0,3,2,1:T(8,128)S(1)}, bf16[2,512,5,64]{1,3,2,0:T(8,128)(2,1)}, bf16[2,512,5,64]{1,3,2,0:T(8,128)(2,1)}, bf16[2,512...) while((s32[]{:T(128)}, f32[128,5,3,64]{0,3,2,1:T(8,128)S(1)}, ...), condition=%wide.region_10.11_spmd.clone, body=%wide.region_9.10_spmd.clone.sunk | while | flops 641540096 | bytes 42503436 | solution.py:248
  271.7 49.8 %reduce-scatter.38.cloned.1.call-done = bf16[128,320]{1,0:T(8,128)(2,1)} async-done(((bf16[1024,320]{1,0:T(8,128)(2,1)}), bf16[128,320]{1,0:T(8,128)(2,1)}) %reduce-scatter.38.cloned.1.call-update) | async-done | bytes 81936
  324.3 62.9 %reduce-scatter.40.cloned.1.call-done = bf16[128,320]{1,0:T(8,128)(2,1)} async-done(((bf16[1024,320]{1,0:T(8,128)(2,1)}), bf16[128,320]{1,0:T(8,128)(2,1)}) %reduce-scatter.40.cloned.1.call-update) | async-done | bytes 81936
  394.3 21.4 %reduce-scatter.28.cloned.1.call-done = bf16[240,640]{1,0:T(8,128)(2,1)} async-done(((bf16[960,640]{1,0:T(8,128)(2,1)}), bf16[240,640]{1,0:T(8,128)(2,1)}) %reduce-scatter.28.cloned.1.call-update) | async-done | bytes 307216 | tf_op jit(solution)/shard_map/reduce_scatter | solution.py:177
  415.7 28.8 %reduce-scatter.30.cloned.1.call-done = bf16[240,640]{1,0:T(8,128)(2,1)} async-done(((bf16[960,640]{1,0:T(8,128)(2,1)}), bf16[240,640]{1,0:T(8,128)(2,1)}) %reduce-scatter.30.cloned.1.call-update) | async-done | bytes 307216 | tf_op jit(solution)/shard_map/reduce_scatter | solution.py:180
  444.5 28.5 %reduce-scatter.32.cloned.1.call-done = bf16[640,240]{0,1:T(8,128)(2,1)} async-done(((bf16[640,960]{0,1:T(8,128)(2,1)}), bf16[640,240]{0,1:T(8,128)(2,1)}) %reduce-scatter.32.cloned.1.call-update) | async-done | bytes 307216 | tf_op jit(solution)/shard_map/reduce_scatter | solution.py:183
  473.7 25.6 %reduce-scatter.42.cloned.1.call-done = bf16[240,320]{1,0:T(8,128)(2,1)} async-done(((bf16[960,320]{1,0:T(8,128)(2,1)}), bf16[240,320]{1,0:T(8,128)(2,1)}) %reduce-scatter.42.cloned.1.call-update) | async-done | bytes 153616
  501.0 24.3 %reduce-scatter.44.cloned.1.call-done = bf16[240,320]{1,0:T(8,128)(2,1)} async-done(((bf16[960,320]{1,0:T(8,128)(2,1)}), bf16[240,320]{1,0:T(8,128)(2,1)}) %reduce-scatter.44.cloned.1.call-update) | async-done | bytes 153616
  527.0 31.5 %reduce-scatter.26.cloned.1.call-done = bf16[240,960]{1,0:T(8,128)(2,1)} async-done(((bf16[960,960]{1,0:T(8,128)(2,1)}), bf16[240,960]{1,0:T(8,128)(2,1)}) %reduce-scatter.26.cloned.1.call-update) | async-done | bytes 460816 | tf_op jit(solution)/shard_map/reduce_scatter | solution.py:313
  558.5 33.0 %reduce-scatter.24.cloned.1.call-done = bf16[240,960]{1,0:T(8,128)(2,1)} async-done(((bf16[960,960]{1,0:T(8,128)(2,1)}), bf16[240,960]{1,0:T(8,128)(2,1)}) %reduce-scatter.24.cloned.1.call-update) | async-done | bytes 460816 | tf_op jit(solution)/shard_map/reduce_scatter | solution.py:304
  596.2 6.0 all-reduce.6
  602.3 16.9 %all-reduce.4 = (bf16[240]{0:T(256)(128)(2,1)S(1)}, bf16[240]{0:T(256)(128)(2,1)S(1)}) all-reduce(bf16[240]{0:T(256)(128)(2,1)S(1)} %dynamic-slice.3, bf16[240]{0:T(256)(128)(2,1)S(1)} %dynamic-slice.5), channel_id=1, replica_groups=mesh['shard'=4,'ctx'=2,'tp'=4] {'ctx','tp'}, use_global_device_ids=true, to_apply=%region_16.17 | all-reduce | flops 480 | bytes 1920 | tf_op jit(solution)/shard_map/psum | solution.py:321
  622.3 8.9 %all-reduce.14.cloned.1.call-done = (bf16[240,640]{1,0:T(8,128)(2,1)}, bf16[240,640]{1,0:T(8,128)(2,1)}, bf16[640,240]{0,1:T(8,128)(2,1)}) async-done(((bf16[240,640]{1,0:T(8,128)(2,1)}, bf16[240,640]{1,0:T(8,128)(2,1)}, bf16[640,240]{0,1:T(8,128)(2,1)}), (bf16[240,640]{1,0:T(8,128)(2,1)}, bf16[240,640]{1,0:T(8,128)(2,1)}, bf16[640,240]{0,1:T(8,128)(2,1)})) %all-reduce.14.cloned.1.call-update) | async-done | bytes 921616 | tf_op jit(solution)/shard_map/psum | solution.py:188
  635.8 84.4 %all-reduce.12.cloned.1.call-done = (bf16[240,960]{1,0:T(8,128)(2,1)}, bf16[240,320]{0,1:T(8,128)(2,1)}, bf16[240,320]{0,1:T(8,128)(2,1)}, bf16[240,960]{1,0:T(8,128)(2,1)}) async-done(((bf16[240,960]{1,0:T(8,128)(2,1)}, bf16[240,320]{0,1:T(8,128)(2,1)}, bf16[240,320]{0,1:T(8,128)(2,1)}, bf16[240,960]{1,0:T(8,128)(2,1)}), (bf16[240,960]{1,0:T(8,128)(2,1)}, bf16[240,320]{0,1:T(8,128)(2,1)}, ...) | async-done | bytes 1228816 | tf_op jit(solution)/shard_map/psum | solution.py:322
  (242 shorter events, 125.5 us)
Async XLA Ops:
  7.2 114.1 %all-gather.8.cloned.1.call-start = ((), (), s32[]{:S(2)}) async-start(), calls=%async_computation.11 | async-start | bytes 2457600 | tf_op jit(solution)/shard_map/all_gather | solution.py:64
  7.9 130.8 %all-gather.10.cloned.1.call-start = ((), (), s32[]{:S(2)}) async-start(), calls=%async_computation.12 | async-start | bytes 2457600 | tf_op jit(solution)/shard_map/all_gather | solution.py:67
  8.7 151.6 %all-gather.12.cloned.1.call-start = ((), (), s32[]{:S(2)}) async-start(), calls=%async_computation.13 | async-start | bytes 1536000 | tf_op jit(solution)/shard_map/all_gather | solution.py:69
  9.4 154.5 %all-gather.14.cloned.1.call-start = ((), (), s32[]{:S(2)}) async-start(), calls=%async_computation.14 | async-start | bytes 1536000 | tf_op jit(solution)/shard_map/all_gather | solution.py:70
  10.0 157.6 %all-gather.16.cloned.1.call-start = ((), (), s32[]{:S(2)}) async-start(), calls=%async_computation.15 | async-start | bytes 1536000 | tf_op jit(solution)/shard_map/all_gather | solution.py:71
  10.6 194.6 %reduce-scatter.36.cloned.1.call-start = ((), (), s32[]{:S(2)}) async-start(), calls=%async_computation.22 | async-start | bytes 1310720
  70.4 31.7 %copy-start.9 = (bf16[960,320]{0,1:T(8,128)(2,1)}, bf16[960,320]{0,1:T(8,128)(2,1)S(1)}, u32[]{:S(2)}) copy-start(bf16[960,320]{0,1:T(8,128)(2,1)S(1)} %reshape.194) | copy-start | bytes 1843204
  178.3 55.1 %reduce-scatter.34.cloned.1.call-start = ((), (), s32[]{:S(2)}) async-start(), calls=%async_computation.21 | async-start | bytes 1310720
  184.1 137.5 %reduce-scatter.38.cloned.1.call-start = ((), (), s32[]{:S(2)}) async-start(), calls=%async_computation.23 | async-start | bytes 884736
  260.0 127.2 %reduce-scatter.40.cloned.1.call-start = ((), (), s32[]{:S(2)}) async-start(), calls=%async_computation.24 | async-start | bytes 884736
  263.1 152.6 %reduce-scatter.28.cloned.1.call-start = ((), (), s32[]{:S(2)}) async-start(), calls=%async_computation.18 | async-start | bytes 1536000 | tf_op jit(solution)/shard_map/reduce_scatter | solution.py:177
  266.3 178.2 %reduce-scatter.30.cloned.1.call-start = ((), (), s32[]{:S(2)}) async-start(), calls=%async_computation.19 | async-start | bytes 1536000 | tf_op jit(solution)/shard_map/reduce_scatter | solution.py:180
  268.4 54.2 %copy-start.3 = (bf16[128,960]{0,1:T(8,128)(2,1)S(1)}, bf16[128,960]{0,1:T(8,128)(2,1)}, u32[]{:S(2)}) copy-start(bf16[128,960]{0,1:T(8,128)(2,1)} %param.16) | copy-start | bytes 737284
  268.4 204.6 %reduce-scatter.32.cloned.1.call-start = ((), (), s32[]{:S(2)}) async-start(), calls=%async_computation.20 | async-start | bytes 1536000 | tf_op jit(solution)/shard_map/reduce_scatter | solution.py:183
  271.6 227.6 %reduce-scatter.42.cloned.1.call-start = ((), (), s32[]{:S(2)}) async-start(), calls=%async_computation.25 | async-start | bytes 921600
  324.2 65.8 %copy-start.7 = (f32[128,960]{0,1:T(8,128)S(1)}, f32[128,960]{0,1:T(8,128)}, u32[]{:S(2)}) copy-start(f32[128,960]{0,1:T(8,128)} %copy-done.6) | copy-start | bytes 1474564
  324.2 65.8 %copy-start.11 = (bf16[128,5,3,64]{0,3,2,1:T(8,128)(2,1)S(1)}, bf16[128,5,3,64]{0,3,2,1:T(8,128)(2,1)}, u32[]{:S(2)}) copy-start(bf16[128,5,3,64]{0,3,2,1:T(8,128)(2,1)} %copy-done.10) | copy-start | bytes 737284
  324.3 201.0 %reduce-scatter.44.cloned.1.call-start = ((), (), s32[]{:S(2)}) async-start(), calls=%async_computation.26 | async-start | bytes 921600
  389.8 168.8 %reduce-scatter.26.cloned.1.call-start = ((), (), s32[]{:S(2)}) async-start(), calls=%async_computation.17 | async-start | bytes 2457600 | tf_op jit(solution)/shard_map/reduce_scatter | solution.py:313
  392.0 199.5 %reduce-scatter.24.cloned.1.call-start = ((), (), s32[]{:S(2)}) async-start(), calls=%async_computation.16 | async-start | bytes 2457600 | tf_op jit(solution)/shard_map/reduce_scatter | solution.py:304
  394.2 237.0 %all-reduce.14.cloned.1.call-start = ((), (), s32[]{:S(2)}) async-start(), calls=%async_computation.28 | async-start | bytes 1843200 | tf_op jit(solution)/shard_map/psum | solution.py:188
  473.0 120.1 %copy-start.20 = (bf16[128,320]{1,0:T(8,128)(2,1)S(1)}, bf16[128,320]{1,0:T(8,128)(2,1)}, u32[]{:S(2)}) copy-start(bf16[128,320]{1,0:T(8,128)(2,1)} %reduce-scatter.40.cloned.1.call-done) | copy-start | bytes 245764
  473.0 247.2 %all-reduce.12.cloned.1.call-start = ((), (), s32[]{:S(2)}) async-start(), calls=%async_computation.27 | async-start | bytes 2621440 | tf_op jit(solution)/shard_map/psum | solution.py:322
  527.0 67.7 %copy-start.4 = (bf16[960,960]{1,0:T(8,128)(2,1)S(1)}, bf16[960,960]{1,0:T(8,128)(2,1)}, u32[]{:S(2)}) copy-start(bf16[960,960]{1,0:T(8,128)(2,1)} %all-gather.8.cloned.1.call-done) | copy-start | bytes 5529604
  (33 other events, 233.5 us)
Sparse Core Ops, SparseCore 0:
  9.6 26.4 all-gather.7
  37.6 21.8 all-gather.9
  61.1 17.7 all-gather.11
  80.3 17.7 all-gather.13
  99.5 17.7 all-gather.15
  178.5 26.6 reduce-scatter.35
  207.6 25.7 reduce-scatter.33
  260.1 61.4 reduce-scatter.37
  325.8 61.3 reduce-scatter.39
  389.6 26.0 reduce-scatter.27
  418.4 26.0 reduce-scatter.29
  446.9 26.0 reduce-scatter.31
  476.3 22.9 reduce-scatter.41
  502.3 23.0 reduce-scatter.43
  527.9 30.6 reduce-scatter.25
  561.0 30.5 reduce-scatter.23
  594.0 37.1 all-reduce.13
  635.5 84.6 all-reduce.11
where the time goes:
time: 736 us; the launch traced here: 733 us
  waiting for transfers between devices  450 us (61%)
  blocking collectives  144 us (20%)
  matrix products  70.2 us (10%)
  local copies, waits for them, and re-layouts  28.3 us (4%)
  other arithmetic  22.7 us (3%)
  between operations  16.2 us (2%)
    unnamed x24, waiting for transfers between devices  214 us
    psum x1, waiting for transfers between devices, per_device(): lax.psum(shard_query.astype(jnp.bfloat16), ('ctx', 'tp'))  84.4 us
    reduce_scatter x1, waiting for transfers between devices, per_device(): lax.psum_scatter(grad_query_w.astype(jnp.bfloat16), 'shard', scatter_dime...  33 us
    reduce_scatter x1, waiting for transfers between devices, per_device(): lax.psum_scatter(grad_out_w.astype(jnp.bfloat16), 'shard', scatter_dimens...  31.5 us
    all_gather x1, blocking collectives, per_device(): lax.all_gather(value_rows, ('ctx', 'tp'), axis=0, tiled=True)  29.9 us
    reduce_scatter x1, waiting for transfers between devices, per_device(): lax.psum_scatter(grad_up_w.astype(jnp.bfloat16), 'shard', scatter_dimensi...  28.8 us
    reduce_scatter x1, waiting for transfers between devices, per_device(): lax.psum_scatter(grad_down_w.astype(jnp.bfloat16), 'shard', scatter_dimen...  28.5 us
    all_gather x1, blocking collectives, per_device(): lax.all_gather(key_row_list, ('ctx', 'tp'), axis=0, tiled=True)  27.4 us
  transfers between devices with their start and end apart: 18, of which 13 were waited for; matrix products, arithmetic and copies ran while one was open for 11% of the time, Pallas kernels for 0%

commit v1 on v0

--- a/solution.py
+++ b/solution.py
@@ -1,8 +1,11 @@
+import functools
 import math
 
 import jax
 import jax.numpy as jnp
 from jax import lax
+from jax.experimental import pallas as pl
+from jax.experimental.pallas import tpu as pltpu
 from jax.sharding import PartitionSpec as P
 
 QUERY_HEADS = 15
@@ -43,6 +46,309 @@
     scaled = grad_normed * gain
     grad_rows = inverse * (scaled - normed * jnp.mean(scaled * normed, axis=-1, keepdims=True))
     return (grad_rows, jnp.sum(grad_normed * normed, axis=0))
+
+
+MESH = pl.DeviceIdType.MESH
+HBM = pl.BlockSpec(memory_space=pl.ANY)
+
+
+def group_size(kind):
+    shard, ctx, tp = lax.axis_size("shard"), lax.axis_size("ctx"), lax.axis_size("tp")
+    return {"core": 2, "x": shard // 2, "shard": shard, "ctx": ctx, "tp": tp, "all": ctx * tp}[kind]
+
+
+def group_place(kind):
+    shard, ctx, tp = lax.axis_index("shard"), lax.axis_index("ctx"), lax.axis_index("tp")
+    if kind == "core":
+        return lax.rem(shard, 2)
+    if kind == "x":
+        return lax.div(shard, 2)
+    if kind == "all":
+        return ctx * lax.axis_size("tp") + tp
+    return {"shard": shard, "ctx": ctx, "tp": tp}[kind]
+
+
+def member(kind, step):
+    size = group_size(kind)
+    place = lax.rem(group_place(kind) + step, size)
+    if kind == "core":
+        return place, {"shard": 2 * lax.div(lax.axis_index("shard"), 2) + place}
+    if kind == "x":
+        return place, {"shard": 2 * place + lax.rem(lax.axis_index("shard"), 2)}
+    if kind == "all":
+        tp = lax.axis_size("tp")
+        return place, {"ctx": lax.div(place, tp), "tp": lax.rem(place, tp)}
+    return place, {kind: place}
+
+
+def greet(kinds):
+    barrier = pltpu.get_barrier_semaphore()
+    total = 0
+    for kind in kinds:
+        for step in range(1, group_size(kind)):
+            _, device = member(kind, step)
+            pl.semaphore_signal(barrier, inc=1, device_id=device, device_id_type=MESH)
+            total += 1
+    pl.semaphore_wait(barrier, total)
+
+
+def send(src, dst, sems, index, device):
+    copy = pltpu.make_async_remote_copy(
+        src_ref=src,
+        dst_ref=dst,
+        send_sem=sems.at[0, index],
+        recv_sem=sems.at[1, index],
+        device_id=device,
+        device_id_type=MESH,
+    )
+    copy.start()
+    return copy
+
+
+def exchange_body(plan, *refs):
+    count = len(plan)
+    ins, outs, sems, local = refs[:count], refs[count : 2 * count], refs[-2], refs[-1]
+    greet(sorted({kind for kind, _ in plan}))
+    copies = []
+    own = []
+    index = 0
+    for item, (kind, mode) in enumerate(plan):
+        me = group_place(kind)
+        if mode == "gather":
+            copy = pltpu.make_async_copy(ins[item], outs[item].at[me], local.at[item])
+            copy.start()
+            own.append(copy)
+    for item, (kind, mode) in enumerate(plan):
+        me = group_place(kind)
+        for step in range(1, group_size(kind)):
+            place, device = member(kind, step)
+            if mode == "gather":
+                source, target = ins[item], outs[item].at[me]
+            elif mode == "second":
+                source, target = ins[item].at[:, place], outs[item].at[step - 1]
+            else:
+                source, target = ins[item].at[place], outs[item].at[step - 1]
+            copies.append(send(source, target, sems, index, device))
+            index += 1
+    for copy in own:
+        copy.wait()
+    for copy in copies:
+        copy.wait()
+
+
+def exchange(collective_id, *items):
+    plan = tuple((kind, mode) for _, kind, mode in items)
+    shapes = []
+    total = 0
+    for array, kind, mode in items:
+        size = group_size(kind)
+        total += size - 1
+        if mode == "gather":
+            shape = (size,) + array.shape
+        elif mode == "second":
+            shape = (size - 1,) + array.shape[:1] + array.shape[2:]
+        else:
+            shape = (size - 1,) + array.shape[1:]
+        shapes.append(jax.ShapeDtypeStruct(shape, array.dtype))
+    return pl.pallas_call(
+        functools.partial(exchange_body, plan),
+        out_shape=shapes,
+        in_specs=[HBM] * len(items),
+        out_specs=[HBM] * len(items),
+        scratch_shapes=[
+            pltpu.SemaphoreType.DMA((2, total)),
+            pltpu.SemaphoreType.DMA((len(items),)),
+        ],
+        compiler_params=pltpu.CompilerParams(collective_id=collective_id, has_side_effects=True),
+    )(*[array for array, _, _ in items])
+
+
+def spread_body(count, *refs):
+    ins, outs, sems, local = refs[:count], refs[count : 2 * count], refs[-2], refs[-1]
+    greet(("ctx", "tp"))
+    ctx, tp = group_place("ctx"), group_place("tp")
+    size_ctx, size_tp = group_size("ctx"), group_size("tp")
+    own = []
+    across = []
+    onward = []
+    index = 0
+    for item in range(count):
+        copy = pltpu.make_async_copy(ins[item], outs[item].at[ctx, tp], local.at[item])
+        copy.start()
+        own.append(copy)
+        for step in range(1, size_tp):
+            _, device = member("tp", step)
+            target = outs[item].at[ctx, tp]
+            across.append((item, step, send(ins[item], target, sems, index, device)))
+            index += 1
+        for hop in range(1, size_ctx):
+            _, device = member("ctx", hop)
+            target = outs[item].at[ctx, tp]
+            onward.append(send(ins[item], target, sems, index, device))
+            index += 1
+    for item, step, copy in across:
+        copy.wait_recv()
+        source = outs[item].at[ctx, lax.rem(tp + size_tp - step, size_tp)]
+        for hop in range(1, size_ctx):
+            _, device = member("ctx", hop)
+            onward.append(send(source, source, sems, index, device))
+            index += 1
+    for _, _, copy in across:
+        copy.wait_send()
+    for copy in onward:
+        copy.wait()
+    for copy in own:
+        copy.wait()
+
+
+def spread(collective_id, *arrays):
+    size_ctx, size_tp = group_size("ctx"), group_size("tp")
+    total = len(arrays) * (size_ctx * size_tp - 1)
+    return pl.pallas_call(
+        functools.partial(spread_body, len(arrays)),
+        out_shape=[
+            jax.ShapeDtypeStruct((size_ctx, size_tp) + array.shape, array.dtype)
+            for array in arrays
+        ],
+        in_specs=[HBM] * len(arrays),
+        out_specs=[HBM] * len(arrays),
+        scratch_shapes=[
+            pltpu.SemaphoreType.DMA((2, total)),
+            pltpu.SemaphoreType.DMA((len(arrays),)),
+        ],
+        compiler_params=pltpu.CompilerParams(collective_id=collective_id, has_side_effects=True),
+    )(*arrays)
+
+
+def pair_device():
+    ctx = lax.axis_index("ctx")
+    return {"ctx": 2 * lax.div(ctx, 2) + 1 - lax.rem(ctx, 2)}
+
+
+def weights_body(halves, *refs):
+    count = len(halves)
+    ins, outs = refs[: count + 2], refs[count + 2 : 2 * count + 4]
+    sems, local = refs[-2], refs[-1]
+    shard, parity = group_place("shard"), lax.rem(lax.axis_index("ctx"), 2)
+    size_x = group_size("x")
+    sibling = member("core", 1)[1]
+    partner = pair_device()
+    barrier = pltpu.get_barrier_semaphore()
+    peers = [sibling, partner]
+    peers += [member("x", step)[1] for step in range(1, size_x)]
+    peers += [member("shard", step)[1] for step in range(1, group_size("shard"))]
+    peers += [member("tp", step)[1] for step in range(1, group_size("tp"))]
+    for device in peers:
+        pl.semaphore_signal(barrier, inc=1, device_id=device, device_id_type=MESH)
+    pl.semaphore_wait(barrier, len(peers))
+
+    def remote(src, dst, index, device):
+        return pltpu.make_async_remote_copy(
+            src_ref=src,
+            dst_ref=dst,
+            send_sem=sems.at[0, index],
+            recv_sem=sems.at[1, index],
+            device_id=device,
+            device_id_type=MESH,
+        )
+
+    plain = []
+    for item in range(count + 2):
+        place = shard if item <= count else group_place("tp")
+        copy = pltpu.make_async_copy(ins[item], outs[item].at[place], local.at[item])
+        copy.start()
+        plain.append(copy)
+    index = 0
+    across = {}
+    for item in range(count):
+        for step in range(1, size_x):
+            _, device = member("x", step)
+            copy = remote(ins[item], outs[item].at[shard], index, device)
+            across[item, step] = copy
+            index += 1
+
+            @pl.when(parity == halves[item])
+            def _():
+                copy.start()
+
+    for step in range(1, group_size("shard")):
+        _, device = member("shard", step)
+        plain.append(send(ins[count], outs[count].at[shard], sems, index, device))
+        index += 1
+    for step in range(1, group_size("tp")):
+        _, device = member("tp", step)
+        target = outs[count + 1].at[group_place("tp")]
+        plain.append(send(ins[count + 1], target, sems, index, device))
+        index += 1
+    for item in range(count):
+        plain.append(send(ins[item], outs[item].at[shard], sems, index, sibling))
+        index += 1
+    handed = {}
+    for step in range(1, size_x):
+        origin = lax.rem(shard + 2 * (size_x - step), 2 * size_x)
+        for item in range(count):
+            block = outs[item].at[origin]
+            handed[item, step] = (
+                remote(block, block, index, partner),
+                remote(block, block, index + 1, sibling),
+            )
+            index += 2
+    for parity_now in range(2):
+
+        @pl.when(parity == parity_now)
+        def _():
+            mine = [key for key in handed if halves[key[0]] == parity_now]
+            others = [key for key in handed if halves[key[0]] != parity_now]
+            for one, two in zip(mine, others):
+                across[one].wait_recv()
+                handed[one][0].start()
+                handed[one][1].start()
+                handed[two][0].wait_recv()
+                handed[two][1].start()
+            for key in mine[len(others) :]:
+                across[key].wait_recv()
+                handed[key][0].start()
+                handed[key][1].start()
+            for key in others[len(mine) :]:
+                handed[key][0].wait_recv()
+                handed[key][1].start()
+            for key in mine:
+                across[key].wait_send()
+                handed[key][0].wait_send()
+
+    for key in handed:
+        handed[key][1].wait()
+    for copy in plain:
+        copy.wait()
+
+
+def gather_weights(collective_id, halves, weights, gains, rows):
+    shard, tp = group_size("shard"), group_size("tp")
+    count = len(weights)
+    total = count * (shard // 2 - 1) * 3 + count + shard - 1 + tp - 1
+    return pl.pallas_call(
+        functools.partial(weights_body, halves),
+        out_shape=[
+            jax.ShapeDtypeStruct((shard,) + array.shape, array.dtype)
+            for array in (*weights, gains)
+        ]
+        + [jax.ShapeDtypeStruct((tp,) + rows.shape, rows.dtype)],
+        in_specs=[HBM] * (count + 2),
+        out_specs=[HBM] * (count + 2),
+        scratch_shapes=[
+            pltpu.SemaphoreType.DMA((2, total)),
+            pltpu.SemaphoreType.DMA((count + 2,)),
+        ],
+        compiler_params=pltpu.CompilerParams(collective_id=collective_id, has_side_effects=True),
+    )(*weights, gains, rows)
+
+
+def total_of(own, others):
+    return own.astype(jnp.float32) + jnp.sum(others.astype(jnp.float32), axis=0)
+
+
+def own_block(array, kind, axis=0):
+    return lax.dynamic_index_in_dim(array, group_place(kind), axis, keepdims=False)
 
 
 def per_device(
@@ -59,17 +365,22 @@
     w_down,
     out_grad,
 ):
-    gain_one, query_w, key_w, value_weight, out_w, gain_two, gate_w, up_w, down_w = (
-        lax.all_gather(norm1_gain, "shard", axis=0, tiled=True),
-        lax.all_gather(w_query, "shard", axis=0, tiled=True),
-        lax.all_gather(w_key, "shard", axis=0, tiled=True),
-        lax.all_gather(w_value, "shard", axis=0, tiled=True),
-        lax.all_gather(w_out, "shard", axis=0, tiled=True),
-        lax.all_gather(norm2_gain, "shard", axis=0, tiled=True),
-        lax.all_gather(w_gate, "shard", axis=0, tiled=True),
-        lax.all_gather(w_up, "shard", axis=0, tiled=True),
-        lax.all_gather(w_down, "shard", axis=1, tiled=True),
-    )
+    piece = norm1_gain.shape[0]
+    gains = jnp.stack([norm1_gain, norm2_gain])
+    gains = jnp.pad(gains, ((0, 14), (0, -piece % 128)))
+    qkv_w, gate_w, out_w, up_w, down_w, gains, grad_all = gather_weights(
+        1,
+        (0, 0, 1, 1, 1),
+        (jnp.concatenate([w_query, w_key, w_value], axis=1), w_gate, w_out, w_up, w_down.T),
+        gains,
+        out_grad,
+    )
+    qkv_w, gate_w, out_w, up_w, down_w, grad_all = (
+        array.reshape(-1, array.shape[-1])
+        for array in (qkv_w, gate_w, out_w, up_w, down_w, grad_all)
+    )
+    gain_one = gains[:, 0, :piece].reshape(-1)
+    gain_two = gains[:, 1, :piece].reshape(-1)
     shard_rows = tokens.shape[0]
     width = tokens.shape[1]
     seq_len = positions.shape[0]
@@ -83,11 +394,10 @@
     residual = tokens.astype(jnp.float32)
     normed_one, inverse_one = norm_rows(residual)
     first_hidden = (normed_one * gain_one).astype(jnp.bfloat16)
-    unrotated_query = jnp.dot(first_hidden, query_w, preferred_element_type=jnp.float32)
-    unrotated_key = jnp.dot(first_hidden, key_w, preferred_element_type=jnp.float32)
-    value_rows = jnp.dot(first_hidden, value_weight, preferred_element_type=jnp.float32).astype(
-        jnp.bfloat16
-    )
+    projected = jnp.dot(first_hidden, qkv_w, preferred_element_type=jnp.float32)
+    unrotated_query = projected[:, :width]
+    unrotated_key = projected[:, width : width + key_value_width]
+    value_rows = projected[:, width + key_value_width :].astype(jnp.bfloat16)
     cosine_table, sine_table = rope_tables(own_place, HEAD_SIZE)
     query_tensor = apply_rotary(
         unrotated_query.reshape(shard_rows, QUERY_HEADS, HEAD_SIZE), cosine_table, sine_table
@@ -97,10 +407,10 @@
         unrotated_key.reshape(shard_rows, KEY_VALUE_HEADS, HEAD_SIZE), cosine_table, sine_table
     ).astype(jnp.bfloat16)
     key_row_list = key_row_list.reshape(shard_rows, key_value_width)
-    gathered_keys, gathered_values = (
-        lax.all_gather(key_row_list, ("ctx", "tp"), axis=0, tiled=True),
-        lax.all_gather(value_rows, ("ctx", "tp"), axis=0, tiled=True),
-    )
+    (gathered,) = spread(2, jnp.concatenate([key_row_list, value_rows], axis=1))
+    gathered = gathered.reshape(seq_len, 2 * key_value_width)
+    gathered_keys = gathered[:, :key_value_width]
+    gathered_values = gathered[:, key_value_width:]
     block_size = 512
     pair_count = seq_len // block_size
     blocked_keys = gathered_keys.reshape(pair_count, block_size, KEY_VALUE_HEADS, HEAD_SIZE)
@@ -144,51 +454,31 @@
     middle = residual + jnp.dot(attention_low, out_w, preferred_element_type=jnp.float32)
     normed_two, inverse_two = norm_rows(middle)
     hidden_two = (normed_two * gain_two).astype(jnp.bfloat16)
-    mlp_input = lax.all_gather(hidden_two, "tp", axis=0, tiled=True)
+    (mlp_input,) = exchange(3, (hidden_two, "tp", "gather"))
+    mlp_input = mlp_input.reshape(-1, width)
     gate = jnp.dot(mlp_input, gate_w, preferred_element_type=jnp.float32)
     upper = jnp.dot(mlp_input, up_w, preferred_element_type=jnp.float32)
     sigma = jax.nn.sigmoid(gate)
     active = gate * sigma
     inner = (active * upper).astype(jnp.bfloat16)
-    mlp_output = lax.psum_scatter(
-        jnp.dot(inner, down_w, preferred_element_type=jnp.float32).astype(jnp.bfloat16),
-        "tp",
-        scatter_dimension=0,
-        tiled=True,
-    ).astype(jnp.float32)
-    result = (middle + mlp_output).astype(jnp.bfloat16)
-    grad_all = lax.all_gather(out_grad, "tp", axis=0, tiled=True)
-    grad_inner = jnp.einsum("rd,fd->rf", grad_all, down_w, preferred_element_type=jnp.float32)
-    grad_down_w = jnp.einsum("rf,rd->fd", inner, grad_all, preferred_element_type=jnp.float32)
+    mlp_output = jnp.einsum("rf,df->rd", inner, down_w, preferred_element_type=jnp.float32)
+    mlp_output = mlp_output.astype(jnp.bfloat16).reshape(-1, shard_rows, width)
+    grad_inner = jnp.einsum("rd,df->rf", grad_all, down_w, preferred_element_type=jnp.float32)
+    grad_down_w = jnp.einsum("rf,rd->df", inner, grad_all, preferred_element_type=jnp.float32)
     grad_gate = (grad_inner * upper * sigma * (1.0 + gate * (1.0 - sigma))).astype(jnp.bfloat16)
     grad_upper = (grad_inner * active).astype(jnp.bfloat16)
     grad_gate_w = jnp.einsum("rd,rf->df", mlp_input, grad_gate, preferred_element_type=jnp.float32)
     grad_up_w = jnp.einsum("rd,rf->df", mlp_input, grad_upper, preferred_element_type=jnp.float32)
-    grad_hidden_two = lax.psum_scatter(
-        (
-            jnp.einsum("rf,df->rd", grad_gate, gate_w, preferred_element_type=jnp.float32)
-            + jnp.einsum("rf,df->rd", grad_upper, up_w, preferred_element_type=jnp.float32)
-        ).astype(jnp.bfloat16),
-        "tp",
-        scatter_dimension=0,
-        tiled=True,
-    ).astype(jnp.float32)
-    shard_gate, shard_up, shard_down = (
-        lax.psum_scatter(
-            grad_gate_w.astype(jnp.bfloat16), "shard", scatter_dimension=0, tiled=True
-        ).astype(jnp.float32),
-        lax.psum_scatter(
-            grad_up_w.astype(jnp.bfloat16), "shard", scatter_dimension=0, tiled=True
-        ).astype(jnp.float32),
-        lax.psum_scatter(
-            grad_down_w.astype(jnp.bfloat16), "shard", scatter_dimension=1, tiled=True
-        ).astype(jnp.float32),
-    )
-    out_gate, out_up, out_down = (
-        lax.psum(shard_gate.astype(jnp.bfloat16), "ctx").astype(jnp.float32),
-        lax.psum(shard_up.astype(jnp.bfloat16), "ctx").astype(jnp.float32),
-        lax.psum(shard_down.astype(jnp.bfloat16), "ctx").astype(jnp.float32),
-    )
+    grad_hidden_two = (
+        jnp.einsum("rf,df->rd", grad_gate, gate_w, preferred_element_type=jnp.float32)
+        + jnp.einsum("rf,df->rd", grad_upper, up_w, preferred_element_type=jnp.float32)
+    ).astype(jnp.bfloat16)
+    grad_hidden_two = grad_hidden_two.reshape(-1, shard_rows, width)
+    hidden_terms, output_terms = exchange(
+        4, (grad_hidden_two, "tp", "first"), (mlp_output, "tp", "first")
+    )
+    grad_hidden_two = total_of(own_block(grad_hidden_two, "tp"), hidden_terms)
+    result = (middle + total_of(own_block(mlp_output, "tp"), output_terms)).astype(jnp.bfloat16)
     grad_middle_norm, grad_gain_two = norm_back(grad_hidden_two, normed_two, inverse_two, gain_two)
     grad_middle = out_grad.astype(jnp.float32) + grad_middle_norm
     grad_middle_low = grad_middle.astype(jnp.bfloat16)
@@ -248,20 +538,17 @@
     grad_query, (key_terms, value_terms) = lax.scan(
         backward_block, query_offset, (blocked_keys, blocked_values, place_blocks)
     )
-    local_key_gradient, grad_value_own = (
-        lax.psum_scatter(
-            key_terms.reshape(seq_len, key_value_width).astype(jnp.bfloat16),
-            ("ctx", "tp"),
-            scatter_dimension=0,
-            tiled=True,
-        ).astype(jnp.float32),
-        lax.psum_scatter(
-            value_terms.reshape(seq_len, key_value_width).astype(jnp.bfloat16),
-            ("ctx", "tp"),
-            scatter_dimension=0,
-            tiled=True,
-        ).astype(jnp.float32),
-    )
+    pair_terms = jnp.concatenate(
+        [
+            key_terms.reshape(-1, shard_rows, key_value_width),
+            value_terms.reshape(-1, shard_rows, key_value_width),
+        ],
+        axis=-1,
+    ).astype(jnp.bfloat16)
+    (other_terms,) = exchange(5, (pair_terms, "all", "first"))
+    pair_grads = total_of(own_block(pair_terms, "all"), other_terms)
+    local_key_gradient = pair_grads[:, :key_value_width]
+    grad_value_own = pair_grads[:, key_value_width:]
     grad_query_raw = (
         apply_rotary(
             grad_query.reshape(shard_rows, QUERY_HEADS, HEAD_SIZE), cosine_table, -sine_table
@@ -279,52 +566,67 @@
         .reshape(shard_rows, key_value_width)
     )
     grad_value_low = grad_value_own.astype(jnp.bfloat16)
-    grad_query_w = jnp.einsum(
-        "rd,rc->dc", first_hidden, grad_query_raw, preferred_element_type=jnp.float32
-    )
-    grad_key_w = jnp.einsum(
-        "rd,rc->dc", first_hidden, grad_key_raw, preferred_element_type=jnp.float32
-    )
-    grad_value_w = jnp.einsum(
-        "rd,rc->dc", first_hidden, grad_value_low, preferred_element_type=jnp.float32
-    )
-    grad_hidden_one = (
-        jnp.einsum("rc,dc->rd", grad_query_raw, query_w, preferred_element_type=jnp.float32)
-        + jnp.einsum("rc,dc->rd", grad_key_raw, key_w, preferred_element_type=jnp.float32)
-        + jnp.einsum("rc,dc->rd", grad_value_low, value_weight, preferred_element_type=jnp.float32)
+    grad_projected = jnp.concatenate([grad_query_raw, grad_key_raw, grad_value_low], axis=1)
+    grad_qkv_w = jnp.einsum(
+        "rd,rc->dc", first_hidden, grad_projected, preferred_element_type=jnp.float32
+    )
+    grad_hidden_one = jnp.einsum(
+        "rc,dc->rd", grad_projected, qkv_w, preferred_element_type=jnp.float32
     )
     grad_residual_norm, grad_gain_one = norm_back(
         grad_hidden_one, normed_one, inverse_one, gain_one
     )
     tokens_grad = (grad_middle + grad_residual_norm).astype(jnp.bfloat16)
-    shard_gain_one, shard_query, shard_key, shard_value, shard_out, shard_gain_two = (
-        lax.psum_scatter(
-            grad_gain_one.astype(jnp.bfloat16), "shard", scatter_dimension=0, tiled=True
-        ).astype(jnp.float32),
-        lax.psum_scatter(
-            grad_query_w.astype(jnp.bfloat16), "shard", scatter_dimension=0, tiled=True
-        ).astype(jnp.float32),
-        lax.psum_scatter(
-            grad_key_w.astype(jnp.bfloat16), "shard", scatter_dimension=0, tiled=True
-        ).astype(jnp.float32),
-        lax.psum_scatter(
-            grad_value_w.astype(jnp.bfloat16), "shard", scatter_dimension=0, tiled=True
-        ).astype(jnp.float32),
-        lax.psum_scatter(
-            grad_out_w.astype(jnp.bfloat16), "shard", scatter_dimension=0, tiled=True
-        ).astype(jnp.float32),
-        lax.psum_scatter(
-            grad_gain_two.astype(jnp.bfloat16), "shard", scatter_dimension=0, tiled=True
-        ).astype(jnp.float32),
-    )
-    out_gain_one, out_query, out_key, out_value, out_proj, out_gain_two = (
-        lax.psum(shard_gain_one.astype(jnp.bfloat16), ("ctx", "tp")).astype(jnp.float32),
-        lax.psum(shard_query.astype(jnp.bfloat16), ("ctx", "tp")).astype(jnp.float32),
-        lax.psum(shard_key.astype(jnp.bfloat16), ("ctx", "tp")).astype(jnp.float32),
-        lax.psum(shard_value.astype(jnp.bfloat16), ("ctx", "tp")).astype(jnp.float32),
-        lax.psum(shard_out.astype(jnp.bfloat16), ("ctx", "tp")).astype(jnp.float32),
-        lax.psum(shard_gain_two.astype(jnp.bfloat16), ("ctx", "tp")).astype(jnp.float32),
-    )
+    size_shard, size_x, size_ctx = group_size("shard"), group_size("x"), group_size("ctx")
+    size_tp = group_size("tp")
+    gain_grads = jnp.stack([grad_gain_one, grad_gain_two]).reshape(2, size_shard, piece)
+    gain_grads = jnp.pad(gain_grads.transpose(1, 0, 2), ((0, 0), (0, 6), (0, -piece % 128)))
+    partial = [
+        array.astype(jnp.bfloat16).reshape(size_x, 2, piece, array.shape[-1])
+        for array in (grad_qkv_w, grad_gate_w, grad_out_w, grad_up_w, grad_down_w)
+    ]
+    *others, other_gains = exchange(
+        6, *[(array, "core", "second") for array in partial], (gain_grads, "shard", "first")
+    )
+    gain_grads = total_of(own_block(gain_grads, "shard"), other_gains)
+    cut = [
+        total_of(own_block(array, "core", 1), other)
+        .astype(jnp.bfloat16)
+        .reshape(size_x, piece, size_ctx, array.shape[-1] // size_ctx)
+        for array, other in zip(partial, others)
+    ]
+    early = jnp.concatenate(cut[:2], axis=-1).transpose(0, 2, 1, 3)
+    late = jnp.concatenate(cut[2:], axis=-1).transpose(2, 0, 1, 3)
+    early_others, late_others, gain_all = exchange(
+        7, (early, "x", "first"), (late, "ctx", "first"), (gain_grads, "all", "gather")
+    )
+    early = total_of(own_block(early, "x"), early_others).astype(jnp.bfloat16)
+    late = total_of(own_block(late, "ctx"), late_others).astype(jnp.bfloat16)
+    early_others, late_others = exchange(8, (early, "ctx", "first"), (late, "x", "first"))
+    early = total_of(own_block(early, "ctx"), early_others)
+    late = total_of(own_block(late, "x"), late_others)
+    qkv_part = qkv_w.shape[-1] // size_ctx
+    out_part = width // size_ctx
+    feed = jnp.concatenate([early[:, qkv_part:], late[:, out_part:]], axis=1).astype(jnp.bfloat16)
+    attend = jnp.concatenate([early[:, :qkv_part], late[:, :out_part]], axis=1)
+    attend = attend.astype(jnp.bfloat16).reshape(piece, size_tp, -1).transpose(1, 0, 2)
+    attend_others, feed = exchange(9, (attend, "tp", "first"), (feed, "ctx", "gather"))
+    attend = total_of(own_block(attend, "tp"), attend_others).astype(jnp.bfloat16)
+    (attend,) = spread(10, attend)
+    attend = attend.transpose(2, 0, 1, 3).reshape(piece, size_ctx, -1).astype(jnp.float32)
+    feed = feed.transpose(1, 0, 2).astype(jnp.float32)
+    out_qkv = attend[:, :, :qkv_part].reshape(piece, -1)
+    out_query = out_qkv[:, :width]
+    out_key = out_qkv[:, width : width + key_value_width]
+    out_value = out_qkv[:, width + key_value_width :]
+    out_proj = attend[:, :, qkv_part:].reshape(piece, -1)
+    hidden_part = gate_w.shape[-1] // size_ctx
+    out_gate = feed[:, :, :hidden_part].reshape(piece, -1)
+    out_up = feed[:, :, hidden_part : 2 * hidden_part].reshape(piece, -1)
+    out_down = feed[:, :, 2 * hidden_part :].reshape(piece, -1).T
+    gain_total = jnp.sum(gain_all, axis=0)
+    out_gain_one = gain_total[0, :piece]
+    out_gain_two = gain_total[1, :piece]
     return (
         result,
         tokens_grad,

time: 736 us -> 505 us (0.69)
  waiting for transfers between devices: 450 us -> 0 us
  Pallas kernels: 0 us -> 304 us
  blocking collectives: 144 us -> 0 us
  local copies, waits for them, and re-layouts: 28.3 us -> 83.8 us
  other arithmetic: 22.7 us -> 51.4 us
  matrix products: 70.2 us -> 55.1 us
  between operations: 16.2 us -> 1.87 us
    pallas_call x0 -> x10, Pallas kernels: none -> 304 us  [the longest x7 180 us: exchange(): pl.pallas_call(functools.partial(exchange_body, plan), out_shape=shapes,...]
    unnamed x24 -> x0, waiting for transfers between devices: 214 us -> none
    reduce_scatter x5 -> x0, waiting for transfers between devices: 143 us -> none  [the longest x1 33 us: per_device(): lax.psum_scatter(grad_query_w.astype(jnp.bfloat16), 'shard', scatter_dime...]
    all_gather x6 -> x0, blocking collectives: 114 us -> none  [the longest x1 29.9 us: per_device(): lax.all_gather(value_rows, ('ctx', 'tp'), axis=0, tiled=True)]
    psum x2 -> x0, waiting for transfers between devices: 93.4 us -> none  [the longest x1 84.4 us: per_device(): lax.psum(shard_query.astype(jnp.bfloat16), ('ctx', 'tp'))]
    psum x1 -> x0, blocking collectives: 16.9 us -> none  [per_device(): lax.psum(shard_gain_one.astype(jnp.bfloat16), ('ctx', 'tp'))]
    convert_element_type x2 -> x13, local copies, waits for them, and re-layouts: 3.53 us -> 19.5 us  [the longest x6 13.1 us: total_of(): return own.astype(jnp.float32) + jnp.sum(others.astype(jnp.float32), axis=0)]
    unnamed x2 -> x0, blocking collectives: 12.9 us -> none
  transfers between devices with their start and end apart: 18 -> 0, of which waited for: 13 -> 0; matrix products, arithmetic and copies ran while one was open for 11% -> 0% of each run, Pallas kernels for 0% -> 0%
where the time goes in v1:
time: 505 us; the launch traced here: 497 us
  Pallas kernels  304 us (60%)
  local copies, waits for them, and re-layouts  83.8 us (17%)
  matrix products  55.1 us (11%)
  other arithmetic  51.4 us (10%)
    pallas_call x7, Pallas kernels, exchange(): pl.pallas_call(functools.partial(exchange_body, plan), out_shape=shapes,...  180 us
    pallas_call x1, Pallas kernels, gather_weights(): pl.pallas_call(functools.partial(weights_body, halves), out_shape=[jax.Sh...  78.4 us
    pallas_call x2, Pallas kernels, spread(): pl.pallas_call(functools.partial(spread_body, len(arrays)), out_shape=[ja...  46 us
    unnamed x128, local copies, waits for them, and re-layouts  20.9 us
    convert_element_type x6, local copies, waits for them, and re-layouts, total_of(): return own.astype(jnp.float32) + jnp.sum(others.astype(jnp.float32), axis=0)  13.1 us
    reduce_sum x6, local copies, waits for them, and re-layouts, total_of(): return own.astype(jnp.float32) + jnp.sum(others.astype(jnp.float32), axis=0)  11.3 us

profile of v1, /device:TPU:20, one launch (start us, length us, event | category | flops | bytes accessed | tf_op | source)
XLA Modules:
  0.0 496.9 jit_solution(6159993981346535682)
XLA Ops:
  8.2 78.4 %shard_map.203 = (bf16[4,240,1600]{2,1,0:T(8,128)(2,1)}, bf16[4,240,640]{2,1,0:T(8,128)(2,1)}, bf16[4,240,960]{2,1,0:T(8,128)(2,1)}, bf16[4,240,640]{2,1,0:T(8,1...) custom-call(bf16[240,1600]{1,0:T(8,128)(2,1)} %concatenate.49.refs_0_, ...), custom_call_target="tpu_custom_call" | custom-call | tf_op jit(solution)/shard_map/pallas_call | solution.py:329
  87.9 3.4 fusion.82
  92.4 20.6 %shard_map.204 = bf16[2,4,128,640]{3,2,1,0:T(8,128)(2,1)} custom-call(bf16[128,640]{1,0:T(8,128)(2,1)} %pad_maximum_fusion.9.refs_0_), custom_call_target="tpu_custom_call" | custom-call | tf_op jit(solution)/shard_map/pallas_call | solution.py:207
  119.4 14.7 %while.30 = (s32[]{:T(128)}, f32[5,3,128]{2,1,0:T(4,128)S(1)}, f32[5,3,128]{2,1,0:T(4,128)S(1)}, f32[5,3,128,64]{2,3,1,0:T(8,128)S(1)}, s32[2,512]{1,0:T(2,128)S...) while((s32[]{:T(128)}, f32[5,3,128]{2,1,0:T(4,128)S(1)}, ...), condition=%wide.region_4.5_spmd.clone, body=%wide.region_1.4_spmd.clone.sunk | while | flops 264881536 | bytes 32427708 | solution.py:448
  122.4 3.2 fusion.160
  129.7 3.2 fusion.160
  138.0 28.5 %shard_map.205 = bf16[4,128,960]{2,1,0:T(8,128)(2,1)} custom-call(bf16[128,960]{1,0:T(8,128)(2,1)} %multiply_convert_fusion.3.refs_0_), custom_call_target="tpu_custom_call" | custom-call | tf_op jit(solution)/shard_map/pallas_call | solution.py:153
  180.9 48.1 %shard_map.206 = (bf16[3,128,960]{2,1,0:T(8,128)(2,1)}, bf16[3,128,960]{2,1,0:T(8,128)(2,1)}) custom-call(bf16[4,128,960]{2,1,0:T(8,128)(2,1)} %bitcast.302, bf16[4,128,960]{2,1,0:T(8,128)(2,1)} %bitcast.306), custom_call_target="tpu_custom_call" | custom-call | tf_op jit(solution)/shard_map/pallas_call | solution.py:153
  236.7 18.5 %while.31 = (s32[]{:T(128)}, f32[128,5,3,64]{0,3,2,1:T(8,128)S(1)}, bf16[2,512,5,64]{1,3,2,0:T(8,128)(2,1)}, bf16[2,512,5,64]{1,3,2,0:T(8,128)(2,1)}, bf16[2,512...) while((s32[]{:T(128)}, f32[128,5,3,64]{0,3,2,1:T(8,128)S(1)}, ...), condition=%wide.region_10.11_spmd.clone, body=%wide.region_9.10_spmd.clone.sunk | while | flops 641540096 | bytes 42503440 | solution.py:538
  241.8 4.0 fusion.177
  251.0 3.9 fusion.177
  262.2 31.2 %shard_map.207 = bf16[7,128,640]{2,1,0:T(8,128)(2,1)} custom-call(bf16[8,128,640]{2,1,0:T(8,128)(2,1)} %pad_maximum_fusion.1.refs_0_), custom_call_target="tpu_custom_call" | custom-call | tf_op jit(solution)/shard_map/pallas_call | solution.py:153
  295.9 3.9 fusion.71
  311.5 8.0 %shard_map.208 = (bf16[1,2,240,1600]{3,2,1,0:T(8,128)(2,1)}, bf16[1,2,240,640]{3,2,1,0:T(8,128)(2,1)}, bf16[1,2,240,960]{3,2,1,0:T(8,128)(2,1)}, bf16[1,2,240,64...) custom-call(bf16[2,2,240,1600]{3,2,1,0:T(8,128)(2,1)} %bitcast.285, ...), custom_call_target="tpu_custom_call" | custom-call | tf_op jit(solution)/shard_map/pallas_call | solution.py:153
  330.7 3.1 copy.150
  338.1 3.0 copy.149
  343.0 4.9 concatenate.60
  347.9 3.9 copy.142
  353.6 4.8 copy.140
  358.4 3.4 add.189
  375.4 30.1 %shard_map.209 = (bf16[1,2,240,1120]{3,2,1,0:T(8,128)(2,1)}, bf16[1,2,240,1120]{3,2,1,0:T(8,128)(2,1)}, f32[8,8,256]{2,1,0:T(8,128)}) custom-call(bf16[2,2,240,1120]{3,2,1,0:T(8,128)(2,1)} %fusion.53.refs_0_, bf16[2,2,240,1120]{3,2,1,0:T(8,128)(2,1)} %bitcast.288, f32[8,256]{1,0:T(8,128)} %fusion.90.refs_2_), custom_call_target="tpu_custom_call" | custom-call | tf_op jit(solution)/shard_map/pallas_call | solution.py:153
  411.1 15.2 %shard_map.210 = (bf16[1,240,1120]{2,1,0:T(8,128)(2,1)}, bf16[1,240,1120]{2,1,0:T(8,128)(2,1)}) custom-call(bf16[2,240,1120]{2,1,0:T(8,128)(2,1)} %bitcast.299, bf16[2,240,1120]{2,1,0:T(8,128)(2,1)} %fusion.54.refs_1_), custom_call_target="tpu_custom_call" | custom-call | tf_op jit(solution)/shard_map/pallas_call | solution.py:153
  430.5 18.6 %shard_map.211 = (bf16[3,240,320]{2,1,0:T(8,128)(2,1)}, bf16[2,240,960]{2,1,0:T(8,128)(2,1)}) custom-call(bf16[4,240,320]{2,1,0:T(8,128)(2,1)} %bitcast.315, bf16[240,960]{1,0:T(8,128)(2,1)} %pad_maximum_fusion.3.refs_1_), custom_call_target="tpu_custom_call" | custom-call | tf_op jit(solution)/shard_map/pallas_call | solution.py:153
  452.0 25.4 %shard_map.212 = bf16[2,4,240,320]{3,2,1,0:T(8,128)(2,1)} custom-call(bf16[240,320]{1,0:T(8,128)(2,1)} %fusion.76.refs_0_), custom_call_target="tpu_custom_call" | custom-call | tf_op jit(solution)/shard_map/pallas_call | solution.py:207
  (306 shorter events, 145.8 us)
Async XLA Ops:
  0.6 6.9 %copy-start.55 = (bf16[240]{0:T(256)(128)(2,1)S(1)}, bf16[240]{0:T(256)(128)(2,1)}, u32[]{:S(2)}) copy-start(bf16[240]{0:T(256)(128)(2,1)} %param.18) | copy-start | bytes 1444
  0.7 6.9 %copy-start.56 = (bf16[240]{0:T(256)(128)(2,1)S(1)}, bf16[240]{0:T(256)(128)(2,1)}, u32[]{:S(2)}) copy-start(bf16[240]{0:T(256)(128)(2,1)} %param.23) | copy-start | bytes 1444
  1.6 253.5 %copy-start.41 = (f32[128,32]{0,1:T(8,128)}, f32[128,32]{0,1:T(8,128)S(1)}, u32[]{:S(2)}) copy-start(f32[128,32]{0,1:T(8,128)S(1)} %get-tuple-element.394) | copy-start | bytes 49156
  5.6 82.0 %copy-start.37 = (bf16[128,960]{0,1:T(8,128)(2,1)S(1)}, bf16[128,960]{0,1:T(8,128)(2,1)}, u32[]{:S(2)}) copy-start(bf16[128,960]{0,1:T(8,128)(2,1)} %param.16) | copy-start | bytes 737284
  87.5 3.7 copy-start.38
  87.7 47.2 %copy-start.5 = (bf16[128,960]{1,0:T(8,128)(2,1)}, bf16[128,960]{1,0:T(8,128)(2,1)S(1)}, u32[]{:S(2)}) copy-start(bf16[128,960]{1,0:T(8,128)(2,1)S(1)} %copy.117) | copy-start | bytes 737284
  87.9 3.4 copy-start.45
  119.7 5.9 %copy-start.31 = (bf16[2,512,5,64]{1,3,2,0:T(8,128)(2,1)S(1)}, bf16[2,512,5,64]{1,3,2,0:T(8,128)(2,1)}, u32[]{:S(2)}) copy-start(bf16[2,512,5,64]{1,3,2,0:T(8,128)(2,1)} %get-tuple-element.570) | copy-start | bytes 1966084 | tf_op jit(solution)/shard_map/while
  122.4 3.3 copy-start
  127.0 5.9 %copy-start.31 = (bf16[2,512,5,64]{1,3,2,0:T(8,128)(2,1)S(1)}, bf16[2,512,5,64]{1,3,2,0:T(8,128)(2,1)}, u32[]{:S(2)}) copy-start(bf16[2,512,5,64]{1,3,2,0:T(8,128)(2,1)} %get-tuple-element.570) | copy-start | bytes 1966084 | tf_op jit(solution)/shard_map/while
  129.6 3.3 copy-start
  134.9 31.6 %copy-start.51 = (bf16[4,240,640]{2,1,0:T(8,128)(2,1)S(1)}, bf16[4,240,640]{2,1,0:T(8,128)(2,1)}, u32[]{:S(2)}) copy-start(bf16[4,240,640]{2,1,0:T(8,128)(2,1)} %get-tuple-element.151) | copy-start | bytes 3686404
  180.9 50.7 %copy-start.14 = (bf16[512,960]{1,0:T(8,128)(2,1)S(1)}, bf16[512,960]{1,0:T(8,128)(2,1)}, u32[]{:S(2)}) copy-start(bf16[512,960]{1,0:T(8,128)(2,1)} %copy.129) | copy-start | bytes 2949124
  229.0 3.4 copy-start.18
  231.6 3.7 copy-start.10
  295.9 4.0 copy-start.44
  295.9 4.7 copy-start.8
  295.9 4.7 copy-start.20
  311.5 9.4 %copy-start.17 = (bf16[960,640]{1,0:T(8,128)(2,1)S(1)}, bf16[960,640]{1,0:T(8,128)(2,1)}, u32[]{:S(2)}) copy-start(bf16[960,640]{1,0:T(8,128)(2,1)} %convolution_convert_fusion.3) | copy-start | bytes 3686404
  347.9 3.9 copy-start.2
  353.6 4.8 copy-start.3
  361.8 5.2 %copy-start.16 = (bf16[960,640]{1,0:T(8,128)(2,1)S(1)}, bf16[960,640]{1,0:T(8,128)(2,1)}, u32[]{:S(2)}) copy-start(bf16[960,640]{1,0:T(8,128)(2,1)} %convolution_convert_fusion.4) | copy-start | bytes 3686404
  411.1 15.2 %copy-start.12 = (bf16[1,2,240,1120]{3,2,1,0:T(8,128)(2,1)S(1)}, bf16[1,2,240,1120]{3,2,1,0:T(8,128)(2,1)}, u32[]{:S(2)}) copy-start(bf16[1,2,240,1120]{3,2,1,0:T(8,128)(2,1)} %fusion.55) | copy-start | bytes 3225604
  411.1 16.6 %copy-start.13 = (bf16[2,240,1120]{2,1,0:T(8,128)(2,1)S(1)}, bf16[2,240,1120]{2,1,0:T(8,128)(2,1)}, u32[]{:S(2)}) copy-start(bf16[2,240,1120]{2,1,0:T(8,128)(2,1)} %fusion.54.refs_1_) | copy-start | bytes 3225604
  (44 other events, 80.1 us)

commit v2 on v1

--- a/solution.py
+++ b/solution.py
@@ -260,16 +260,24 @@
         plain.append(copy)
     index = 0
     across = {}
+    pieces = 3 if ins[0].shape[0] % 48 == 0 else 1
+    height = ins[0].shape[0] // pieces
     for item in range(count):
-        for step in range(1, size_x):
-            _, device = member("x", step)
-            copy = remote(ins[item], outs[item].at[shard], index, device)
-            across[item, step] = copy
-            index += 1
-
-            @pl.when(parity == halves[item])
-            def _():
-                copy.start()
+        for part in range(pieces):
+            cut = pl.ds(part * height, height)
+            for step in range(1, size_x):
+                _, device = member("x", step)
+                target = outs[item].at[shard, cut]
+                across[item, part, step] = remote(ins[item].at[cut], target, index, device)
+                index += 1
+    ahead = 3 * (size_x - 1)
+    for parity_now in range(2):
+
+        @pl.when(parity == parity_now)
+        def _():
+            mine = [key for key in across if halves[key[0]] == parity_now]
+            for key in mine[:ahead]:
+                across[key].start()
 
     for step in range(1, group_size("shard")):
         _, device = member("shard", step)
@@ -284,36 +292,35 @@
         plain.append(send(ins[item], outs[item].at[shard], sems, index, sibling))
         index += 1
     handed = {}
-    for step in range(1, size_x):
+    for item, part, step in across:
         origin = lax.rem(shard + 2 * (size_x - step), 2 * size_x)
-        for item in range(count):
-            block = outs[item].at[origin]
-            handed[item, step] = (
-                remote(block, block, index, partner),
-                remote(block, block, index + 1, sibling),
-            )
-            index += 2
+        block = outs[item].at[origin, pl.ds(part * height, height)]
+        handed[item, part, step] = (
+            remote(block, block, index, partner),
+            remote(block, block, index + 1, sibling),
+        )
+        index += 2
+    lag = 2
     for parity_now in range(2):
 
         @pl.when(parity == parity_now)
         def _():
             mine = [key for key in handed if halves[key[0]] == parity_now]
             others = [key for key in handed if halves[key[0]] != parity_now]
-            for one, two in zip(mine, others):
-                across[one].wait_recv()
-                handed[one][0].start()
-                handed[one][1].start()
-                handed[two][0].wait_recv()
-                handed[two][1].start()
-            for key in mine[len(others) :]:
-                across[key].wait_recv()
-                handed[key][0].start()
-                handed[key][1].start()
-            for key in others[len(mine) :]:
-                handed[key][0].wait_recv()
-                handed[key][1].start()
+            for turn in range(max(len(mine), len(others) + lag)):
+                if turn < len(mine):
+                    key = mine[turn]
+                    across[key].wait_recv()
+                    handed[key][0].start()
+                    handed[key][1].start()
+                    across[key].wait_send()
+                    if turn + ahead < len(mine):
+                        across[mine[turn + ahead]].start()
+                if lag <= turn < len(others) + lag:
+                    key = others[turn - lag]
+                    handed[key][0].wait_recv()
+                    handed[key][1].start()
             for key in mine:
-                across[key].wait_send()
                 handed[key][0].wait_send()
 
     for key in handed:
@@ -325,7 +332,8 @@
 def gather_weights(collective_id, halves, weights, gains, rows):
     shard, tp = group_size("shard"), group_size("tp")
     count = len(weights)
-    total = count * (shard // 2 - 1) * 3 + count + shard - 1 + tp - 1
+    pieces = 3 if weights[0].shape[0] % 48 == 0 else 1
+    total = count * pieces * (shard // 2 - 1) * 3 + count + shard - 1 + tp - 1
     return pl.pallas_call(
         functools.partial(weights_body, halves),
         out_shape=[
@@ -341,6 +349,220 @@
         ],
         compiler_params=pltpu.CompilerParams(collective_id=collective_id, has_side_effects=True),
     )(*weights, gains, rows)
+
+
+def reduce_body(sizes, *refs):
+    attn, gate, up, down, gains, terms, attn_out, feed_out, gain_out, terms_in = refs[:10]
+    from_core, feed_core, attn_x, attn_x_in, attn_sum, attn_ctx_in, attn_part = refs[10:17]
+    attn_tp_in, feed_sum, feed_ctx_in, feed_mid, feed_x_in, gain_in, gain_sum, sems = refs[17:]
+    piece, padded = sizes
+    size_x, size_ctx, size_tp = group_size("x"), group_size("ctx"), group_size("tp")
+    size_shard, size_all = group_size("shard"), group_size("all")
+    rows, columns = padded // size_ctx, attn.shape[-1] // size_tp
+    feeds = (gate, up, down)
+    hidden = gate.shape[-1]
+    x, core, ctx, tp = (group_place(kind) for kind in ("x", "core", "ctx", "tp"))
+    shard, all_place = group_place("shard"), group_place("all")
+    greet(("shard", "all"))
+    used = []
+
+    def start(src, dst, device):
+        copy = send(src, dst, sems, len(used), device)
+        used.append(copy)
+        return copy
+
+    def arrived(copies):
+        for copy in copies:
+            copy.wait_recv()
+
+    def add(target, *terms):
+        total = terms[0].astype(jnp.float32)
+        for term in terms[1:]:
+            total = total + term.astype(jnp.float32)
+        return total.astype(target.dtype)
+
+    other, sibling = member("core", 1)
+    attn_core = [
+        start(attn.at[2 * block + other], from_core.at[block], sibling) for block in range(size_x)
+    ]
+    feed_core_copies = [
+        start(
+            feeds[item].at[2 * block + other],
+            feed_core.at[item, block],
+            sibling,
+        )
+        for item in range(3)
+        for block in range(size_x)
+    ]
+    gain_copies = []
+    for step in range(1, size_shard):
+        place, device = member("shard", step)
+        gain_copies.append(start(gains.at[place], gain_in.at[step - 1], device))
+    term_copies = []
+    for step in range(1, size_tp):
+        place, device = member("tp", step)
+        term_copies.append(start(terms.at[place], terms_in.at[step - 1], device))
+
+    if padded > piece:
+        attn_x[:, piece:, :] = jnp.zeros((size_x, padded - piece, attn.shape[-1]), attn.dtype)
+        feed_sum[:, piece:, :] = jnp.zeros((size_x, padded - piece, 3 * hidden), attn.dtype)
+    arrived(attn_core)
+    for block in range(size_x):
+        for at in range(0, attn.shape[-1], 640):
+            cut = slice(at, at + 640)
+            attn_x[block, :piece, cut] = add(
+                attn_x, attn[2 * block + core, :, cut], from_core[block, :, cut]
+            )
+    attn_x_copies = []
+    for step in range(1, size_x):
+        place, device = member("x", step)
+        attn_x_copies.append(start(attn_x.at[place], attn_x_in.at[step - 1], device))
+
+    arrived(feed_core_copies)
+    for item in range(3):
+        for block in range(size_x):
+            cut = slice(item * hidden, (item + 1) * hidden)
+            feed_sum[block, :piece, cut] = add(
+                feed_sum, feeds[item][2 * block + core], feed_core[item, block]
+            )
+    feed_ctx_copies = []
+    for step in range(1, size_ctx):
+        place, device = member("ctx", step)
+        first = pl.multiple_of(place * rows, rows)
+        feed_ctx_copies.append(
+            start(feed_sum.at[:, pl.ds(first, rows)], feed_ctx_in.at[step - 1], device)
+        )
+    my_rows = pl.ds(pl.multiple_of(ctx * rows, rows), rows)
+
+    arrived(gain_copies)
+    gain_sum[...] = gains[shard] + jnp.sum(gain_in[...], axis=0)
+    gain_out[all_place] = gain_sum[...]
+    gain_last = []
+    for step in range(1, size_all):
+        _, device = member("all", step)
+        gain_last.append(start(gain_sum, gain_out.at[all_place], device))
+
+    arrived(feed_ctx_copies)
+    for at in range(0, 3 * hidden, 640):
+        cut = slice(at, at + 640)
+        for block in range(size_x):
+            feed_mid[block, :, cut] = add(
+                feed_mid,
+                feed_sum[block, my_rows, cut],
+                *[feed_ctx_in[step, block, :, cut] for step in range(size_ctx - 1)],
+            )
+    feed_x_copies = []
+    for step in range(1, size_x):
+        place, device = member("x", step)
+        feed_x_copies.append(start(feed_mid.at[place], feed_x_in.at[step - 1], device))
+
+    arrived(attn_x_copies)
+    for at in range(0, attn.shape[-1], 640):
+        cut = slice(at, at + 640)
+        attn_sum[:, cut] = add(
+            attn_sum, attn_x[x, :, cut], *[attn_x_in[step, :, cut] for step in range(size_x - 1)]
+        )
+    attn_ctx_copies = []
+    for step in range(1, size_ctx):
+        place, device = member("ctx", step)
+        first = pl.multiple_of(place * rows, rows)
+        attn_ctx_copies.append(
+            start(attn_sum.at[pl.ds(first, rows)], attn_ctx_in.at[step - 1], device)
+        )
+
+    arrived(attn_ctx_copies)
+    for part in range(size_tp):
+        cut = slice(part * columns, (part + 1) * columns)
+        attn_part[part] = add(
+            attn_part,
+            attn_sum[my_rows, cut],
+            *[attn_ctx_in[step, :, cut] for step in range(size_ctx - 1)],
+        )
+    attn_tp_copies = []
+    for step in range(1, size_tp):
+        place, device = member("tp", step)
+        attn_tp_copies.append(start(attn_part.at[place], attn_tp_in.at[step - 1], device))
+
+    arrived(feed_x_copies)
+    for at in range(0, 3 * hidden, 640):
+        cut = slice(at, at + 640)
+        feed_out[ctx, :, cut] = add(
+            feed_out, feed_mid[x, :, cut], *[feed_x_in[step, :, cut] for step in range(size_x - 1)]
+        )
+    feed_last = []
+    for step in range(1, size_ctx):
+        _, device = member("ctx", step)
+        feed_last.append(start(feed_out.at[ctx], feed_out.at[ctx], device))
+
+    arrived(attn_tp_copies)
+    attn_out[ctx, tp] = add(
+        attn_out, attn_part[tp], *[attn_tp_in[step] for step in range(size_tp - 1)]
+    )
+    mine = attn_out.at[ctx, tp]
+    across = []
+    last = []
+    for step in range(1, size_tp):
+        _, device = member("tp", step)
+        across.append((step, start(mine, mine, device)))
+    for hop in range(1, size_ctx):
+        _, device = member("ctx", hop)
+        last.append(start(mine, mine, device))
+    for step, copy in across:
+        copy.wait_recv()
+        block = attn_out.at[ctx, lax.rem(tp + size_tp - step, size_tp)]
+        for hop in range(1, size_ctx):
+            _, device = member("ctx", hop)
+            last.append(start(block, block, device))
+    arrived(last)
+    arrived(feed_last)
+    arrived(gain_last)
+    arrived(term_copies)
+    for copy in used:
+        copy.wait_send()
+
+
+def reduce_weights(collective_id, attn, gate, up, down, gains, terms):
+    size_shard, size_x, size_ctx = group_size("shard"), group_size("x"), group_size("ctx")
+    size_tp, size_all = group_size("tp"), group_size("all")
+    piece, width, hidden = attn.shape[1], attn.shape[2], gate.shape[2]
+    unit = 16 * size_ctx
+    padded = -(-piece // unit) * unit
+    rows, columns = padded // size_ctx, width // size_tp
+    low = attn.dtype
+    total = 4 * size_x + size_shard - 1 + 2 * (size_x - 1) + 3 * (size_ctx - 1)
+    total += 2 * (size_all - 1) + 2 * (size_tp - 1)
+    vmem = pl.BlockSpec(memory_space=pltpu.VMEM)
+    return pl.pallas_call(
+        functools.partial(reduce_body, (piece, padded)),
+        out_shape=[
+            jax.ShapeDtypeStruct((size_ctx, size_tp, rows, columns), low),
+            jax.ShapeDtypeStruct((size_ctx, rows, 3 * hidden), low),
+            jax.ShapeDtypeStruct((size_all,) + gains.shape[1:], gains.dtype),
+            jax.ShapeDtypeStruct((size_tp - 1,) + terms.shape[1:], terms.dtype),
+        ],
+        in_specs=[vmem] * 5 + [HBM],
+        out_specs=[vmem] * 3 + [HBM],
+        scratch_shapes=[
+            pltpu.VMEM((size_x, piece, width), low),
+            pltpu.VMEM((3, size_x, piece, hidden), low),
+            pltpu.VMEM((size_x, padded, width), low),
+            pltpu.VMEM((size_x - 1, padded, width), low),
+            pltpu.VMEM((padded, width), low),
+            pltpu.VMEM((size_ctx - 1, rows, width), low),
+            pltpu.VMEM((size_tp, rows, columns), low),
+            pltpu.VMEM((size_tp - 1, rows, columns), low),
+            pltpu.VMEM((size_x, padded, 3 * hidden), low),
+            pltpu.VMEM((size_ctx - 1, size_x, rows, 3 * hidden), low),
+            pltpu.VMEM((size_x, rows, 3 * hidden), low),
+            pltpu.VMEM((size_x - 1, rows, 3 * hidden), low),
+            pltpu.VMEM((size_shard - 1,) + gains.shape[1:], gains.dtype),
+            pltpu.VMEM(gains.shape[1:], gains.dtype),
+            pltpu.SemaphoreType.DMA((2, total)),
+        ],
+        compiler_params=pltpu.CompilerParams(
+            collective_id=collective_id, has_side_effects=True, vmem_limit_bytes=56 * 2**20
+        ),
+    )(attn, gate, up, down, gains, terms)
 
 
 def total_of(own, others):
@@ -474,11 +696,8 @@
         + jnp.einsum("rf,df->rd", grad_upper, up_w, preferred_element_type=jnp.float32)
     ).astype(jnp.bfloat16)
     grad_hidden_two = grad_hidden_two.reshape(-1, shard_rows, width)
-    hidden_terms, output_terms = exchange(
-        4, (grad_hidden_two, "tp", "first"), (mlp_output, "tp", "first")
-    )
+    (hidden_terms,) = exchange(4, (grad_hidden_two, "tp", "first"))
     grad_hidden_two = total_of(own_block(grad_hidden_two, "tp"), hidden_terms)
-    result = (middle + total_of(own_block(mlp_output, "tp"), output_terms)).astype(jnp.bfloat16)
     grad_middle_norm, grad_gain_two = norm_back(grad_hidden_two, normed_two, inverse_two, gain_two)
     grad_middle = out_grad.astype(jnp.float32) + grad_middle_norm
     grad_middle_low = grad_middle.astype(jnp.bfloat16)
@@ -577,53 +796,34 @@
         grad_hidden_one, normed_one, inverse_one, gain_one
     )
     tokens_grad = (grad_middle + grad_residual_norm).astype(jnp.bfloat16)
-    size_shard, size_x, size_ctx = group_size("shard"), group_size("x"), group_size("ctx")
-    size_tp = group_size("tp")
+    size_shard = group_size("shard")
     gain_grads = jnp.stack([grad_gain_one, grad_gain_two]).reshape(2, size_shard, piece)
     gain_grads = jnp.pad(gain_grads.transpose(1, 0, 2), ((0, 0), (0, 6), (0, -piece % 128)))
-    partial = [
-        array.astype(jnp.bfloat16).reshape(size_x, 2, piece, array.shape[-1])
-        for array in (grad_qkv_w, grad_gate_w, grad_out_w, grad_up_w, grad_down_w)
-    ]
-    *others, other_gains = exchange(
-        6, *[(array, "core", "second") for array in partial], (gain_grads, "shard", "first")
-    )
-    gain_grads = total_of(own_block(gain_grads, "shard"), other_gains)
-    cut = [
-        total_of(own_block(array, "core", 1), other)
-        .astype(jnp.bfloat16)
-        .reshape(size_x, piece, size_ctx, array.shape[-1] // size_ctx)
-        for array, other in zip(partial, others)
-    ]
-    early = jnp.concatenate(cut[:2], axis=-1).transpose(0, 2, 1, 3)
-    late = jnp.concatenate(cut[2:], axis=-1).transpose(2, 0, 1, 3)
-    early_others, late_others, gain_all = exchange(
-        7, (early, "x", "first"), (late, "ctx", "first"), (gain_grads, "all", "gather")
-    )
-    early = total_of(own_block(early, "x"), early_others).astype(jnp.bfloat16)
-    late = total_of(own_block(late, "ctx"), late_others).astype(jnp.bfloat16)
-    early_others, late_others = exchange(8, (early, "ctx", "first"), (late, "x", "first"))
-    early = total_of(own_block(early, "ctx"), early_others)
-    late = total_of(own_block(late, "x"), late_others)
-    qkv_part = qkv_w.shape[-1] // size_ctx
-    out_part = width // size_ctx
-    feed = jnp.concatenate([early[:, qkv_part:], late[:, out_part:]], axis=1).astype(jnp.bfloat16)
-    attend = jnp.concatenate([early[:, :qkv_part], late[:, :out_part]], axis=1)
-    attend = attend.astype(jnp.bfloat16).reshape(piece, size_tp, -1).transpose(1, 0, 2)
-    attend_others, feed = exchange(9, (attend, "tp", "first"), (feed, "ctx", "gather"))
-    attend = total_of(own_block(attend, "tp"), attend_others).astype(jnp.bfloat16)
-    (attend,) = spread(10, attend)
-    attend = attend.transpose(2, 0, 1, 3).reshape(piece, size_ctx, -1).astype(jnp.float32)
-    feed = feed.transpose(1, 0, 2).astype(jnp.float32)
-    out_qkv = attend[:, :, :qkv_part].reshape(piece, -1)
-    out_query = out_qkv[:, :width]
-    out_key = out_qkv[:, width : width + key_value_width]
-    out_value = out_qkv[:, width + key_value_width :]
-    out_proj = attend[:, :, qkv_part:].reshape(piece, -1)
-    hidden_part = gate_w.shape[-1] // size_ctx
-    out_gate = feed[:, :, :hidden_part].reshape(piece, -1)
-    out_up = feed[:, :, hidden_part : 2 * hidden_part].reshape(piece, -1)
-    out_down = feed[:, :, 2 * hidden_part :].reshape(piece, -1).T
+    grad_attention_w = jnp.concatenate(
+        [grad_qkv_w.astype(jnp.bfloat16), grad_out_w.astype(jnp.bfloat16)], axis=1
+    )
+    attention_total, feed_total, gain_all, output_terms = reduce_weights(
+        6,
+        *[
+            array.astype(jnp.bfloat16).reshape(size_shard, piece, array.shape[-1])
+            for array in (grad_attention_w, grad_gate_w, grad_up_w, grad_down_w)
+        ],
+        gain_grads,
+        mlp_output,
+    )
+    result = (middle + total_of(own_block(mlp_output, "tp"), output_terms)).astype(jnp.bfloat16)
+    attention_total = attention_total.transpose(0, 2, 1, 3).reshape(-1, grad_attention_w.shape[1])
+    attention_total = attention_total[:piece].astype(jnp.float32)
+    feed_total = feed_total.reshape(-1, feed_total.shape[-1])[:piece].astype(jnp.float32)
+    projected_width = width + 2 * key_value_width
+    hidden_part = gate_w.shape[-1]
+    out_query = attention_total[:, :width]
+    out_key = attention_total[:, width : width + key_value_width]
+    out_value = attention_total[:, width + key_value_width : projected_width]
+    out_proj = attention_total[:, projected_width:]
+    out_gate = feed_total[:, :hidden_part]
+    out_up = feed_total[:, hidden_part : 2 * hidden_part]
+    out_down = feed_total[:, 2 * hidden_part :].T
     gain_total = jnp.sum(gain_all, axis=0)
     out_gain_one = gain_total[0, :piece]
     out_gain_two = gain_total[1, :piece]

time: 505 us -> 409 us (0.81)
  local copies, waits for them, and re-layouts: 83.8 us -> 34.6 us
  other arithmetic: 51.4 us -> 24.5 us
  Pallas kernels: 304 us -> 285 us
    pallas_call x0 -> x1, Pallas kernels: none -> 101 us  [reduce_weights(): pl.pallas_call(functools.partial(reduce_body, (piece, padded)), out_shape...]
    pallas_call x7 -> x3, Pallas kernels: 180 us -> 85.2 us  [exchange(): pl.pallas_call(functools.partial(exchange_body, plan), out_shape=shapes,...]
    pallas_call x2 -> x1, Pallas kernels: 46 us -> 20.6 us  [spread(): pl.pallas_call(functools.partial(spread_body, len(arrays)), out_shape=[ja...]
    convert_element_type x8 -> x0, local copies, waits for them, and re-layouts: 16.6 us -> none  [the longest x6 13.1 us: total_of(): return own.astype(jnp.float32) + jnp.sum(others.astype(jnp.float32), axis=0)]
    convert_element_type x10 -> x3, other arithmetic: 17.6 us -> 1.45 us  [the longest x1 1.05 us: per_device(): (middle + total_of(own_block(mlp_output, 'tp'), output_terms)).astype(jnp...]
    reduce_sum x6 -> x0, local copies, waits for them, and re-layouts: 11.3 us -> none  [total_of(): return own.astype(jnp.float32) + jnp.sum(others.astype(jnp.float32), axis=0)]
    unnamed x128 -> x80, local copies, waits for them, and re-layouts: 20.9 us -> 12.7 us
    add x6 -> x1, other arithmetic: 7.28 us -> 0.11 us  [total_of(): return own.astype(jnp.float32) + jnp.sum(others.astype(jnp.float32), axis=0)]
where the time goes in v2:
time: 409 us; the launch traced here: 403 us
  Pallas kernels  285 us (70%)
  matrix products  56.1 us (14%)
  local copies, waits for them, and re-layouts  34.6 us (8%)
  other arithmetic  24.5 us (6%)
    pallas_call x1, Pallas kernels, reduce_weights(): pl.pallas_call(functools.partial(reduce_body, (piece, padded)), out_shape...  101 us
    pallas_call x3, Pallas kernels, exchange(): pl.pallas_call(functools.partial(exchange_body, plan), out_shape=shapes,...  85.2 us
    pallas_call x1, Pallas kernels, gather_weights(): pl.pallas_call(functools.partial(weights_body, halves), out_shape=[jax.Sh...  79 us
    pallas_call x1, Pallas kernels, spread(): pl.pallas_call(functools.partial(spread_body, len(arrays)), out_shape=[ja...  20.6 us
    unnamed x80, local copies, waits for them, and re-layouts  12.7 us

profile of v2, /device:TPU:20, one launch (start us, length us, event | category | flops | bytes accessed | tf_op | source)
XLA Modules:
  0.0 403.0 jit_solution(17832247801656269072)
XLA Ops:
  8.8 79.0 %shard_map.203 = (bf16[4,240,1600]{2,1,0:T(8,128)(2,1)}, bf16[4,240,640]{2,1,0:T(8,128)(2,1)}, bf16[4,240,960]{2,1,0:T(8,128)(2,1)}, bf16[4,240,640]{2,1,0:T(8,1...) custom-call(bf16[240,1600]{1,0:T(8,128)(2,1)} %concatenate.38.refs_0_, ...), custom_call_target="tpu_custom_call" | custom-call | tf_op jit(solution)/shard_map/pallas_call | solution.py:337
  89.0 3.4 fusion.74
  93.5 20.6 %shard_map.204 = bf16[2,4,128,640]{3,2,1,0:T(8,128)(2,1)} custom-call(bf16[128,640]{1,0:T(8,128)(2,1)} %pad_maximum_fusion.7.refs_0_), custom_call_target="tpu_custom_call" | custom-call | tf_op jit(solution)/shard_map/pallas_call | solution.py:207
  121.4 14.9 %while.30 = (s32[]{:T(128)}, f32[5,3,128]{2,1,0:T(4,128)S(1)}, f32[5,3,128]{2,1,0:T(4,128)S(1)}, f32[5,3,128,64]{2,3,1,0:T(8,128)S(1)}, s32[2,512]{1,0:T(2,128)S...) while((s32[]{:T(128)}, f32[5,3,128]{2,1,0:T(4,128)S(1)}, ...), condition=%wide.region_4.5_spmd.clone, body=%wide.region_1.4_spmd.clone.sunk | while | flops 264881536 | bytes 29806240 | solution.py:670
  121.7 2.7 fusion.149
  124.5 3.2 fusion.150
  129.1 2.7 fusion.149
  131.8 3.2 fusion.150
  136.4 2.2 multiply_reduce_fusion.2
  139.5 28.5 %shard_map.205 = bf16[4,128,960]{2,1,0:T(8,128)(2,1)} custom-call(bf16[128,960]{1,0:T(8,128)(2,1)} %multiply_convert_fusion.3.refs_0_), custom_call_target="tpu_custom_call" | custom-call | tf_op jit(solution)/shard_map/pallas_call | solution.py:153
  168.0 2.7 fusion.90
  177.9 25.5 %shard_map.206 = bf16[3,128,960]{2,1,0:T(8,128)(2,1)} custom-call(bf16[4,128,960]{2,1,0:T(8,128)(2,1)} %bitcast.243), custom_call_target="tpu_custom_call" | custom-call | tf_op jit(solution)/shard_map/pallas_call | solution.py:153
  207.1 2.4 convolution_convert_fusion.6
  209.7 20.1 %while.31 = (s32[]{:T(128)}, f32[128,5,3,64]{0,3,2,1:T(8,128)S(1)}, bf16[2,512,5,64]{1,3,2,0:T(8,128)(2,1)}, bf16[2,512,5,64]{1,3,2,0:T(8,128)(2,1)}, bf16[2,512...) while((s32[]{:T(128)}, f32[128,5,3,64]{0,3,2,1:T(8,128)S(1)}, ...), condition=%wide.region_9.10_spmd.clone, body=%wide.region_8.9_spmd.clone.sunk | while | flops 641540096 | bytes 42503436 | solution.py:757
  210.9 2.7 fusion.164
  215.7 4.0 fusion.167
  220.8 2.7 fusion.164
  225.6 4.0 fusion.167
  236.9 31.2 %shard_map.207 = bf16[7,128,640]{2,1,0:T(8,128)(2,1)} custom-call(bf16[8,128,640]{2,1,0:T(8,128)(2,1)} %pad_maximum_fusion.1.refs_0_), custom_call_target="tpu_custom_call" | custom-call | tf_op jit(solution)/shard_map/pallas_call | solution.py:153
  270.6 3.8 fusion.60
  277.1 3.7 pad_maximum_fusion
  287.4 3.1 convolution_convert_fusion.2
  290.5 100.5 %shard_map.208 = (bf16[2,4,128,640]{3,2,1,0:T(8,128)(2,1)}, bf16[2,128,1920]{2,1,0:T(8,128)(2,1)}, f32[8,8,256]{2,1,0:T(8,128)}, bf16[3,128,960]{2,1,0:T(8,128)(2,1)}) custom-call(bf16[4,240,2560]{2,1,0:T(8,128)(2,1)} %bitcast.239, bf16[4,240,640]{2,1,0:T(8,128)(2,1)} %bitcast.257, bf16[4,240,640]{2,1,0:T(8,128)(2,1)} %bitcast.258, ...), custom_call_target="tpu_custom_call" | custom-call | tf_op jit(solution)/shard_map/pallas_call | solution.py:535
  391.0 2.3 copy.112
  (206 shorter events, 66.3 us)
Async XLA Ops:
  0.6 7.5 %copy-start.31 = (bf16[240]{0:T(256)(128)(2,1)S(1)}, bf16[240]{0:T(256)(128)(2,1)}, u32[]{:S(2)}) copy-start(bf16[240]{0:T(256)(128)(2,1)} %param.18) | copy-start | bytes 1444
  0.7 7.5 %copy-start.32 = (bf16[240]{0:T(256)(128)(2,1)S(1)}, bf16[240]{0:T(256)(128)(2,1)}, u32[]{:S(2)}) copy-start(bf16[240]{0:T(256)(128)(2,1)} %param.23) | copy-start | bytes 1444
  6.1 82.5 %copy-start.21 = (bf16[128,960]{0,1:T(8,128)(2,1)S(1)}, bf16[128,960]{0,1:T(8,128)(2,1)}, u32[]{:S(2)}) copy-start(bf16[128,960]{0,1:T(8,128)(2,1)} %param.16) | copy-start | bytes 737284
  88.8 47.5 %copy-start.4 = (bf16[128,960]{1,0:T(8,128)(2,1)}, bf16[128,960]{1,0:T(8,128)(2,1)S(1)}, u32[]{:S(2)}) copy-start(bf16[128,960]{1,0:T(8,128)(2,1)S(1)} %copy.88) | copy-start | bytes 737284
  92.4 21.7 %copy-start.8 = (f32[128,1600]{0,1:T(8,128)}, f32[128,1600]{0,1:T(8,128)S(1)}, u32[]{:S(2)}) copy-start(f32[128,1600]{0,1:T(8,128)S(1)} %fusion.74) | copy-start | bytes 2457604
  124.4 3.3 copy-start
  131.8 3.3 copy-start
  136.3 31.6 %copy-start.10 = (bf16[128,5,3,64]{0,3,2,1:T(8,128)(2,1)}, bf16[128,5,3,64]{0,3,2,1:T(8,128)(2,1)S(1)}, u32[]{:S(2)}) copy-start(bf16[128,5,3,64]{0,3,2,1:T(8,128)(2,1)S(1)} %bitcast_convert_fusion) | copy-start | bytes 737284
  138.5 67.4 %copy-start.2 = (f32[128,960]{1,0:T(8,128)}, f32[128,960]{1,0:T(8,128)S(1)}, u32[]{:S(2)}) copy-start(f32[128,960]{1,0:T(8,128)S(1)} %get-tuple-element.376) | copy-start | bytes 1474564
  167.9 2.8 copy-start.25
  167.9 2.8 copy-start.29
  172.3 2.2 copy-start.28
  177.9 28.1 %copy-start.9 = (bf16[128,960]{1,0:T(8,128)(2,1)S(1)}, bf16[128,960]{1,0:T(8,128)(2,1)}, u32[]{:S(2)}) copy-start(bf16[128,960]{1,0:T(8,128)(2,1)} %copy.91.refs_6_) | copy-start | bytes 737284
  207.1 2.6 copy-start.6
  209.7 20.2 %copy-start.22 = (f32[128,32]{0,1:T(8,128)S(1)}, f32[128,32]{0,1:T(8,128)}, u32[]{:S(2)}) copy-start(f32[128,32]{0,1:T(8,128)} %get-tuple-element.372) | copy-start | bytes 49156
  210.5 3.2 copy-start.1
  215.6 4.0 copy-start.15
  220.4 3.2 copy-start.1
  225.6 4.0 copy-start.15
  277.0 3.7 copy-start.13
  277.0 3.7 copy-start.36
  280.7 2.0 copy-start.34
  282.8 2.0 copy-start.37
  399.0 2.9 copy-start.23
  (20 other events, 24.7 us)
